TPU v7x, 32 devices: a whole 2x2x4 slice. The times are simulated.
32 devices in a mesh: rad: 2 (over y), az: 16 (over z, x, core).
Axes of the slice: x: 2, y: 2, z: 4, core: 2. Of those that a mesh axis runs over, the one named last changes fastest.
Arguments:
- dust_density: float32 [128, 256, 128], P('rad', 'az'), may hold values from 0.05 to 1
- dust_velocity: float32 [128, 256, 2, 128], P('rad', 'az'), may hold values from -6 to 6
- gas_density: float32 [256, 1024], P('rad', 'az'), may hold values from 0.5 to 2
- gas_velocity: float32 [256, 2, 1024], P('rad', None, 'az'), may hold values from -6 to 6
- kernel: float32 [128, 128], replicated, may hold values from 0.0005 to 0.005
- grain_param: float32 [128], replicated, may hold values from 0.1 to 10
- cycle_shifts: int32 [128], P('rad'), may hold values from 0 to 255
- fragment_bins: int32 [128, 128], replicated, may hold values from 0 to 127
- gas_map: int32 [128], P('rad'), may hold values from 0 to 255, as said below
Outputs:
- dust_density_out: float32 [128, 256, 128], P('rad', 'az')
- dust_velocity_out: float32 [128, 256, 2, 128], P('rad', 'az')
- gas_velocity_out: float32 [256, 2, 1024], P('rad', None, 'az')
Inputs may be any that keep to these rules, and one draw needn't show every extreme that they name: gas_map never decreases along the dust cycles; the first dust cycle maps to gas cycle 0 and the last to gas cycle 256 - 1. `gas_map`: the dust cycles of index i of rad map into gas cycles of index i - 1 or i of rad, and each index after the first has a dust cycle in the gas cycles of index i - 1.
All inputs are finite; a program needn't handle non-finite values.
Results may differ from a plain program's by a relative error of at most 0.000064.
Values sent between devices are 32-bit elements; how exact they have to be, the bound alone decides.
A program may use at most 64 MiB of HBM per device.

v0:
```python
import math

import jax
import jax.numpy as jnp
from jax import lax
from jax.sharding import PartitionSpec as P


def shifted(block, axis, distance):
    devices = range(lax.axis_size(axis))
    route = [(i - distance, i) for i in devices if i - distance in devices]
    return lax.ppermute(block, axis, route)


def body(
    dust_density,
    dust_velocity,
    gas_density,
    gas_velocity,
    kernel,
    grain_param,
    cycle_shifts,
    fragment_bins,
    gas_map,
):
    cycles, cells, bins = dust_density.shape
    gas_cycles = gas_density.shape[0]
    state = jnp.concatenate([dust_density[:, :, None, :], dust_velocity], axis=2)
    whole = lax.all_to_all(state, "az", split_axis=0, concat_axis=1, tiled=True)
    owned = whole.shape[0]
    full_cells = whole.shape[1]
    local_shift = lax.dynamic_slice_in_dim(cycle_shifts, lax.axis_index("az") * owned, owned)
    position = (
        jnp.arange(full_cells, dtype=jnp.int32)[None, :] - local_shift[:, None]
    ) % full_cells
    turned = jnp.take_along_axis(whole, position[:, :, None, None], axis=1)
    state = lax.all_to_all(turned, "az", split_axis=1, concat_axis=0, tiled=True)
    moved_density = state[:, :, 0, :]
    moved_velocity = state[:, :, 1:, :]
    onehot = (
        fragment_bins.reshape(-1)[:, None] == jnp.arange(bins, dtype=jnp.int32)[None, :]
    ).astype(jnp.float32)
    table = kernel.reshape(-1)[:, None] * onehot
    total_cells = cycles * cells
    block = math.gcd(total_cells, 64)

    def coag_block(dens):
        pairs = (dens[:, :, None] * dens[:, None, :]).reshape(dens.shape[0], -1)
        gain = jnp.dot(pairs, table, precision=lax.Precision.HIGHEST)
        loss = dens * jnp.dot(dens, kernel.T, precision=lax.Precision.HIGHEST)
        return dens + gain - loss

    coag_density = lax.map(
        coag_block, moved_density.reshape(total_cells // block, block, bins)
    ).reshape(cycles, cells, bins)
    coarse_density = gas_density.reshape(gas_cycles, cells, 4).mean(-1)
    coarse_velocity = (
        gas_velocity.reshape(gas_cycles, 2, cells, 4).mean(-1).reshape(gas_cycles, 2 * cells)
    )
    prev_density, prev_velocity = shifted((coarse_density, coarse_velocity), "rad", 1)
    near_density = jnp.concatenate([prev_density, coarse_density], axis=0)
    near_velocity = jnp.concatenate([prev_velocity, coarse_velocity], axis=0)
    first_row = (lax.axis_index("rad") - 1) * gas_cycles
    near_rows = first_row + jnp.arange(2 * gas_cycles, dtype=jnp.int32)
    select = (gas_map[:, None] == near_rows[None, :]).astype(jnp.float32)
    rho_dust = jnp.dot(select, near_density, precision=lax.Precision.HIGHEST)
    u_flat = jnp.dot(select, near_velocity, precision=lax.Precision.HIGHEST)
    u_dust = jnp.transpose(u_flat.reshape(cycles, 2, cells), (0, 2, 1))
    frac = 1.0 - jnp.exp(-rho_dust[:, :, None] / grain_param[None, None, :])
    velocity_out = moved_velocity + (u_dust[:, :, :, None] - moved_velocity) * frac[:, :, None, :]
    momentum = jnp.sum(coag_density[:, :, None, :] * (velocity_out - moved_velocity), axis=3) / bins
    spread = jnp.repeat(jnp.transpose(momentum, (0, 2, 1)), 4, axis=2).reshape(cycles, 8 * cells)
    near_kick = jnp.dot(select.T, spread, precision=lax.Precision.HIGHEST)
    from_next = shifted(near_kick[:gas_cycles], "rad", -1)
    kick = (near_kick[gas_cycles:] + from_next).reshape(gas_cycles, 2, 4 * cells)
    gas_out = gas_velocity - kick / gas_density[:, None, :]
    return (coag_density, velocity_out, gas_out)


def solution(mesh):
    placed = (
        P("rad", "az", None),
        P("rad", "az", None, None),
        P("rad", "az"),
        P("rad", None, "az"),
        P(),
        P(),
        P("rad"),
        P(),
        P("rad"),
    )
    return jax.shard_map(
        body,
        mesh=mesh,
        in_specs=placed,
        out_specs=(P("rad", "az", None), P("rad", "az", None, None), P("rad", None, "az")),
        check_vma=False,
    )
```

profile of v0, /device:TPU:10, one launch (start us, length us, event | category | flops | bytes accessed | tf_op | source)
XLA Modules:
  0.0 466.4 jit_solution(5631672533702118456)
XLA Ops:
  0.6 1.4 copy.36
  2.0 1.3 pad_maximum_fusion
  3.3 6.4 %all-to-all-start = ((f32[64,16,3,128]{3,1,2,0:T(8,128)}), f32[64,16,3,128]{3,1,2,0:T(8,128)S(1)}, u32[]{:S(2)}, u32[]{:S(2)}) async-start(f32[64,16,3,128]{3,1,2,0:T(8,128)} %pad_maximum_fusion), calls=%async_computation | async-start | bytes 3145728 | tf_op jit(solution)/shard_map/all_to_all | solution.py:29
  9.9 35.7 %all-to-all-done = f32[64,16,3,128]{3,1,2,0:T(8,128)S(1)} async-done(((f32[64,16,3,128]{3,1,2,0:T(8,128)}), f32[64,16,3,128]{3,1,2,0:T(8,128)S(1)}, u32[]{:S(2)}, u32[]{:S(2)}) %all-to-all-start) | async-done | bytes 1572896 | tf_op jit(solution)/shard_map/all_to_all | solution.py:29
  45.8 2.4 copy.38
  48.2 6.2 %gather_fusion = f32[1024,3,128]{2,1,0:T(4,128)S(1)} fusion(f32[4,256,3,128]{3,2,1,0:T(4,128)} %copy.38, s32[1024]{0:T(1024)S(1)} %bitcast.56), kind=kCustom, calls=%fused_computation | custom fusion | bytes 3153920 | tf_op jit(solution)/shard_map/jit(take_along_axis)/gather | solution.py:36
  54.4 2.1 copy_select_fusion
  56.5 5.2 %all-to-all-start.1 = ((f32[4,256,3,128]{3,0,2,1:T(4,128)}), f32[4,256,3,128]{3,0,2,1:T(4,128)S(1)}, u32[]{:S(2)}, u32[]{:S(2)}) async-start(f32[4,256,3,128]{3,0,2,1:T(4,128)} %copy_select_fusion), calls=%async_computation.1 | async-start | bytes 3145728 | tf_op jit(solution)/shard_map/all_to_all | solution.py:37
  61.7 3.4 collective-permute-start.1
  65.3 1.3 collective-permute-start
  68.3 29.4 %all-to-all-done.1 = f32[4,256,3,128]{3,0,2,1:T(4,128)S(1)} async-done(((f32[4,256,3,128]{3,0,2,1:T(4,128)}), f32[4,256,3,128]{3,0,2,1:T(4,128)S(1)}, u32[]{:S(2)}, u32[]{:S(2)}) %all-to-all-start.1) | async-done | bytes 1572896 | tf_op jit(solution)/shard_map/all_to_all | solution.py:37
  98.7 358.6 %while.11 = (s32[]{:T(128)}, f32[16,64,128]{2,1,0:T(8,128)}, f32[16,64,128]{2,1,0:T(8,128)S(1)}, f32[128,128]{1,0:T(8,128)S(1)}, s32[16384]{0:T(1024)S(1)}, /*index=5*/f32[16384]{0:T(1024)S(1)}, s32[]{:T(128)}) while((s32[]{:T(128)}, f32[16,64,128]{2,1,0:T(8,128)}, f32[16,64,128]{2,1,0:T(8,128)S(1)}, f32[128,128]{1,0:T(8,128)S(1)}, ...), condition=%wide.region_1.2_spmd.clone, body=%wide.region_0.1_spmd.clone.sunk | while | flops 1628463104 | bytes 8880721 | solution.py:53
  99.9 20.4 %fusion.60 = f32[64,128]{1,0:T(8,128)S(1)} fusion(f32[64,128]{1,0:T(8,128)S(1)} %dynamic-slice_bitcast_fusion.2, f32[16384]{0:T(1024)S(1)} %get-tuple-element.126, s32[16384]{0:T(1024)S(1)} %get-tuple-element.125, f32[8,8,128,128]{3,2,1,0:T(8,128)S(1)} %bitcast.55), kind=kOutput, calls=%fused_computation.15.clone.1 | convolution fusion | flops 1614815232 | bytes 4390912 | tf_op jit(solution)/shard_map/while/body/eval_jaxpr/dot_general | solution.py:49
  122.3 20.4 %fusion.60 = f32[64,128]{1,0:T(8,128)S(1)} fusion(f32[64,128]{1,0:T(8,128)S(1)} %dynamic-slice_bitcast_fusion.2, f32[16384]{0:T(1024)S(1)} %get-tuple-element.126, s32[16384]{0:T(1024)S(1)} %get-tuple-element.125, f32[8,8,128,128]{3,2,1,0:T(8,128)S(1)} %bitcast.55), kind=kOutput, calls=%fused_computation.15.clone.1 | convolution fusion | flops 1614815232 | bytes 4390912 | tf_op jit(solution)/shard_map/while/body/eval_jaxpr/dot_general | solution.py:49
  144.7 20.4 %fusion.60 = f32[64,128]{1,0:T(8,128)S(1)} fusion(f32[64,128]{1,0:T(8,128)S(1)} %dynamic-slice_bitcast_fusion.2, f32[16384]{0:T(1024)S(1)} %get-tuple-element.126, s32[16384]{0:T(1024)S(1)} %get-tuple-element.125, f32[8,8,128,128]{3,2,1,0:T(8,128)S(1)} %bitcast.55), kind=kOutput, calls=%fused_computation.15.clone.1 | convolution fusion | flops 1614815232 | bytes 4390912 | tf_op jit(solution)/shard_map/while/body/eval_jaxpr/dot_general | solution.py:49
  167.1 20.4 %fusion.60 = f32[64,128]{1,0:T(8,128)S(1)} fusion(f32[64,128]{1,0:T(8,128)S(1)} %dynamic-slice_bitcast_fusion.2, f32[16384]{0:T(1024)S(1)} %get-tuple-element.126, s32[16384]{0:T(1024)S(1)} %get-tuple-element.125, f32[8,8,128,128]{3,2,1,0:T(8,128)S(1)} %bitcast.55), kind=kOutput, calls=%fused_computation.15.clone.1 | convolution fusion | flops 1614815232 | bytes 4390912 | tf_op jit(solution)/shard_map/while/body/eval_jaxpr/dot_general | solution.py:49
  189.5 20.4 %fusion.60 = f32[64,128]{1,0:T(8,128)S(1)} fusion(f32[64,128]{1,0:T(8,128)S(1)} %dynamic-slice_bitcast_fusion.2, f32[16384]{0:T(1024)S(1)} %get-tuple-element.126, s32[16384]{0:T(1024)S(1)} %get-tuple-element.125, f32[8,8,128,128]{3,2,1,0:T(8,128)S(1)} %bitcast.55), kind=kOutput, calls=%fused_computation.15.clone.1 | convolution fusion | flops 1614815232 | bytes 4390912 | tf_op jit(solution)/shard_map/while/body/eval_jaxpr/dot_general | solution.py:49
  212.0 20.4 %fusion.60 = f32[64,128]{1,0:T(8,128)S(1)} fusion(f32[64,128]{1,0:T(8,128)S(1)} %dynamic-slice_bitcast_fusion.2, f32[16384]{0:T(1024)S(1)} %get-tuple-element.126, s32[16384]{0:T(1024)S(1)} %get-tuple-element.125, f32[8,8,128,128]{3,2,1,0:T(8,128)S(1)} %bitcast.55), kind=kOutput, calls=%fused_computation.15.clone.1 | convolution fusion | flops 1614815232 | bytes 4390912 | tf_op jit(solution)/shard_map/while/body/eval_jaxpr/dot_general | solution.py:49
  234.4 20.4 %fusion.60 = f32[64,128]{1,0:T(8,128)S(1)} fusion(f32[64,128]{1,0:T(8,128)S(1)} %dynamic-slice_bitcast_fusion.2, f32[16384]{0:T(1024)S(1)} %get-tuple-element.126, s32[16384]{0:T(1024)S(1)} %get-tuple-element.125, f32[8,8,128,128]{3,2,1,0:T(8,128)S(1)} %bitcast.55), kind=kOutput, calls=%fused_computation.15.clone.1 | convolution fusion | flops 1614815232 | bytes 4390912 | tf_op jit(solution)/shard_map/while/body/eval_jaxpr/dot_general | solution.py:49
  256.8 20.4 %fusion.60 = f32[64,128]{1,0:T(8,128)S(1)} fusion(f32[64,128]{1,0:T(8,128)S(1)} %dynamic-slice_bitcast_fusion.2, f32[16384]{0:T(1024)S(1)} %get-tuple-element.126, s32[16384]{0:T(1024)S(1)} %get-tuple-element.125, f32[8,8,128,128]{3,2,1,0:T(8,128)S(1)} %bitcast.55), kind=kOutput, calls=%fused_computation.15.clone.1 | convolution fusion | flops 1614815232 | bytes 4390912 | tf_op jit(solution)/shard_map/while/body/eval_jaxpr/dot_general | solution.py:49
  279.2 20.4 %fusion.60 = f32[64,128]{1,0:T(8,128)S(1)} fusion(f32[64,128]{1,0:T(8,128)S(1)} %dynamic-slice_bitcast_fusion.2, f32[16384]{0:T(1024)S(1)} %get-tuple-element.126, s32[16384]{0:T(1024)S(1)} %get-tuple-element.125, f32[8,8,128,128]{3,2,1,0:T(8,128)S(1)} %bitcast.55), kind=kOutput, calls=%fused_computation.15.clone.1 | convolution fusion | flops 1614815232 | bytes 4390912 | tf_op jit(solution)/shard_map/while/body/eval_jaxpr/dot_general | solution.py:49
  301.6 20.4 %fusion.60 = f32[64,128]{1,0:T(8,128)S(1)} fusion(f32[64,128]{1,0:T(8,128)S(1)} %dynamic-slice_bitcast_fusion.2, f32[16384]{0:T(1024)S(1)} %get-tuple-element.126, s32[16384]{0:T(1024)S(1)} %get-tuple-element.125, f32[8,8,128,128]{3,2,1,0:T(8,128)S(1)} %bitcast.55), kind=kOutput, calls=%fused_computation.15.clone.1 | convolution fusion | flops 1614815232 | bytes 4390912 | tf_op jit(solution)/shard_map/while/body/eval_jaxpr/dot_general | solution.py:49
  324.0 20.4 %fusion.60 = f32[64,128]{1,0:T(8,128)S(1)} fusion(f32[64,128]{1,0:T(8,128)S(1)} %dynamic-slice_bitcast_fusion.2, f32[16384]{0:T(1024)S(1)} %get-tuple-element.126, s32[16384]{0:T(1024)S(1)} %get-tuple-element.125, f32[8,8,128,128]{3,2,1,0:T(8,128)S(1)} %bitcast.55), kind=kOutput, calls=%fused_computation.15.clone.1 | convolution fusion | flops 1614815232 | bytes 4390912 | tf_op jit(solution)/shard_map/while/body/eval_jaxpr/dot_general | solution.py:49
  346.4 20.4 %fusion.60 = f32[64,128]{1,0:T(8,128)S(1)} fusion(f32[64,128]{1,0:T(8,128)S(1)} %dynamic-slice_bitcast_fusion.2, f32[16384]{0:T(1024)S(1)} %get-tuple-element.126, s32[16384]{0:T(1024)S(1)} %get-tuple-element.125, f32[8,8,128,128]{3,2,1,0:T(8,128)S(1)} %bitcast.55), kind=kOutput, calls=%fused_computation.15.clone.1 | convolution fusion | flops 1614815232 | bytes 4390912 | tf_op jit(solution)/shard_map/while/body/eval_jaxpr/dot_general | solution.py:49
  368.8 20.4 %fusion.60 = f32[64,128]{1,0:T(8,128)S(1)} fusion(f32[64,128]{1,0:T(8,128)S(1)} %dynamic-slice_bitcast_fusion.2, f32[16384]{0:T(1024)S(1)} %get-tuple-element.126, s32[16384]{0:T(1024)S(1)} %get-tuple-element.125, f32[8,8,128,128]{3,2,1,0:T(8,128)S(1)} %bitcast.55), kind=kOutput, calls=%fused_computation.15.clone.1 | convolution fusion | flops 1614815232 | bytes 4390912 | tf_op jit(solution)/shard_map/while/body/eval_jaxpr/dot_general | solution.py:49
  391.3 20.4 %fusion.60 = f32[64,128]{1,0:T(8,128)S(1)} fusion(f32[64,128]{1,0:T(8,128)S(1)} %dynamic-slice_bitcast_fusion.2, f32[16384]{0:T(1024)S(1)} %get-tuple-element.126, s32[16384]{0:T(1024)S(1)} %get-tuple-element.125, f32[8,8,128,128]{3,2,1,0:T(8,128)S(1)} %bitcast.55), kind=kOutput, calls=%fused_computation.15.clone.1 | convolution fusion | flops 1614815232 | bytes 4390912 | tf_op jit(solution)/shard_map/while/body/eval_jaxpr/dot_general | solution.py:49
  413.7 20.4 %fusion.60 = f32[64,128]{1,0:T(8,128)S(1)} fusion(f32[64,128]{1,0:T(8,128)S(1)} %dynamic-slice_bitcast_fusion.2, f32[16384]{0:T(1024)S(1)} %get-tuple-element.126, s32[16384]{0:T(1024)S(1)} %get-tuple-element.125, f32[8,8,128,128]{3,2,1,0:T(8,128)S(1)} %bitcast.55), kind=kOutput, calls=%fused_computation.15.clone.1 | convolution fusion | flops 1614815232 | bytes 4390912 | tf_op jit(solution)/shard_map/while/body/eval_jaxpr/dot_general | solution.py:49
  436.1 20.4 %fusion.60 = f32[64,128]{1,0:T(8,128)S(1)} fusion(f32[64,128]{1,0:T(8,128)S(1)} %dynamic-slice_bitcast_fusion.2, f32[16384]{0:T(1024)S(1)} %get-tuple-element.126, s32[16384]{0:T(1024)S(1)} %get-tuple-element.125, f32[8,8,128,128]{3,2,1,0:T(8,128)S(1)} %bitcast.55), kind=kOutput, calls=%fused_computation.15.clone.1 | convolution fusion | flops 1614815232 | bytes 4390912 | tf_op jit(solution)/shard_map/while/body/eval_jaxpr/dot_general | solution.py:49
  457.3 1.7 multiply_reduce_fusion
  459.5 1.3 collective-permute-start.2
  460.8 1.5 copy.45
  462.3 3.4 collective-permute-done.2
  (92 shorter events, 36.4 us)
Async XLA Ops:
  0.6 1.4 copy-start.1
  3.3 6.4 %copy-start.7 = (s32[64]{0:T(128)S(1)}, s32[64]{0:T(128)}, u32[]{:S(2)}) copy-start(s32[64]{0:T(128)} %param.17) | copy-start | bytes 772
  3.3 42.4 %all-to-all-start = ((f32[64,16,3,128]{3,1,2,0:T(8,128)}), f32[64,16,3,128]{3,1,2,0:T(8,128)S(1)}, u32[]{:S(2)}, u32[]{:S(2)}) async-start(f32[64,16,3,128]{3,1,2,0:T(8,128)} %pad_maximum_fusion), calls=%async_computation | async-start | bytes 3145728 | tf_op jit(solution)/shard_map/all_to_all | solution.py:29
  56.5 5.2 %copy-start.3 = (f32[128,64]{0,1:T(8,128)S(1)}, f32[128,64]{0,1:T(8,128)}, u32[]{:S(2)}) copy-start(f32[128,64]{0,1:T(8,128)} %param.13) | copy-start | bytes 98308
  56.5 8.7 %copy-start.2 = (f32[128,2,64]{0,2,1:T(8,128)S(1)}, f32[128,2,64]{0,2,1:T(8,128)}, u32[]{:S(2)}) copy-start(f32[128,2,64]{0,2,1:T(8,128)} %param.14) | copy-start | bytes 196612
  56.5 10.1 %copy-start.5 = (s32[64]{0:T(128)S(1)}, s32[64]{0:T(128)}, u32[]{:S(2)}) copy-start(s32[64]{0:T(128)} %param.19) | copy-start | bytes 772
  56.5 10.4 %copy-start.4 = (f32[128]{0:T(128)S(1)}, f32[128]{0:T(128)}, u32[]{:S(2)}) copy-start(f32[128]{0:T(128)} %param.16) | copy-start | bytes 1540
  56.5 41.2 %all-to-all-start.1 = ((f32[4,256,3,128]{3,0,2,1:T(4,128)}), f32[4,256,3,128]{3,0,2,1:T(4,128)S(1)}, u32[]{:S(2)}, u32[]{:S(2)}) async-start(f32[4,256,3,128]{3,0,2,1:T(4,128)} %copy_select_fusion), calls=%async_computation.1 | async-start | bytes 3145728 | tf_op jit(solution)/shard_map/all_to_all | solution.py:37
  61.7 4.9 %collective-permute-start.1 = (f32[128,16]{0,1:T(8,128)S(1)}, f32[128,16]{0,1:T(8,128)S(1)}, u32[]{:S(2)}, u32[]{:S(2)}) collective-permute-start(f32[128,16]{0,1:T(8,128)S(1)} %broadcast_multiply_fusion.2), channel_id=1, source_target_pairs={{0,16},{1,17},{2,18},{3,19},{4,20},{5,21},{6,22},{7,23},{8,24},{9,... | collective-permute-start | bytes 24584 | tf_op jit(solution)/shard_map/ppermute | solution.py:12
  65.3 2.7 collective-permute-start
  97.9 0.8 copy-start
  97.9 0.9 copy-start.6
  459.5 6.2 %collective-permute-start.2 = (f32[128,128]{0,1:T(8,128)S(1)}, f32[128,128]{0,1:T(8,128)S(1)}, u32[]{:S(2)}, u32[]{:S(2)}) collective-permute-start(f32[128,128]{0,1:T(8,128)S(1)} %slice.21), channel_id=1, source_target_pairs={{16,0},{17,1},{18,2},{19,3},{20,4},{21,5},{22,6},{23,7},{24,8},{25... | collective-permute-start | bytes 196616 | tf_op jit(solution)/shard_map/ppermute | solution.py:12
where the time goes:
time: 467 us; the launch traced here: 466 us
  matrix products  341 us (73%)
  waiting for transfers between devices  69.4 us (15%)
  other arithmetic  24.5 us (5%)
  starting transfers between devices  17.6 us (4%)
  local copies, waits for them, and re-layouts  13 us (3%)
    dot_general x16, matrix products, coag_block(): gain = jnp.dot(pairs, table, precision=lax.Precision.HIGHEST)  326 us
    all_to_all x1, waiting for transfers between devices, body(): whole = lax.all_to_all(state, 'az', split_axis=0, concat_axis=1, tiled=True)  35.7 us
    all_to_all x1, waiting for transfers between devices, body(): lax.all_to_all(turned, 'az', split_axis=1, concat_axis=0, tiled=True)  29.4 us
    mul x16, other arithmetic, coag_block(): pairs = (dens[:, :, None] * dens[:, None, :]).reshape(dens.shape[0], -1)  18.3 us
    dot_general x16, matrix products, coag_block(): loss = dens * jnp.dot(dens, kernel.T, precision=lax.Precision.HIGHEST)  13.9 us
  transfers between devices with their start and end apart: 5, of which 4 were waited for; matrix products, arithmetic and copies ran while one was open for 1% of the time, Pallas kernels for 0%

commit v1 on v0

v1 whole, which is shorter than its diff:
```python
import functools

import jax
import jax.numpy as jnp
from jax import lax
from jax.experimental import pallas as pl
from jax.experimental.pallas import tpu as pltpu
from jax.sharding import PartitionSpec as P

F32 = jnp.float32
BF16 = jnp.bfloat16
VMEM = pl.BlockSpec(memory_space=pltpu.VMEM)
SMEM = pl.BlockSpec(memory_space=pltpu.SMEM)
GROUP = 6
ABT = (((1,), (1,)), ((), ()))


def split_parts(x):
    hi = x.astype(BF16)
    return hi, (x - hi.astype(F32)).astype(BF16)


def diagonals(x):
    n = x.shape[0]
    lane = lax.broadcasted_iota(jnp.int32, x.shape, 1)
    step = 1
    while step < n:
        x = jnp.where((lane & step) != 0, pltpu.roll(x, n - step, 0), x)
        step *= 2
    return x


def coag_kernel(dens_ref, rate_ref, bins_ref, out_ref, rates, places, acc):
    n = rate_ref.shape[0]
    half = n // 2
    rate = rate_ref[...]
    place = bins_ref[...].astype(F32)
    dist = lax.broadcasted_iota(jnp.int32, (n, n), 0)
    rates[0] = jnp.where(dist <= half, diagonals(rate.T), 0.0)
    rates[1] = jnp.where((dist > 0) & (dist < half), diagonals(rate), 0.0)
    places[0] = diagonals(place.T)
    places[1] = diagonals(place)

    dens = dens_ref[...]
    hi, lo = split_parts(dens)
    rate_hi, rate_lo = split_parts(rate)
    both = jnp.concatenate([rate_hi, rate_lo], axis=0)
    lost = lax.dot_general(
        jnp.concatenate([hi, lo], axis=1),
        jnp.concatenate([both, both], axis=1),
        ABT,
        preferred_element_type=F32,
    )
    out_ref[...] = dens - dens * (lost[:, :n] + lost[:, n:])
    acc[...] = jnp.zeros_like(acc)
    bin_id = lax.broadcasted_iota(jnp.int32, (n, n), 0).astype(F32)

    def step(g, carry):
        table_hi, table_lo, pair_hi, pair_lo = [], [], [], []
        for t in range(GROUP):
            d = g * GROUP + t
            row = pl.ds(d, 1)
            table = jnp.where(bin_id == places[0, row, :], rates[0, row, :], 0.0) + jnp.where(
                bin_id == places[1, row, :], rates[1, row, :], 0.0
            )
            h, l = split_parts(table)
            table_hi.append(h)
            table_lo.append(l)
            x = dens_ref[...]
            h, l = split_parts(x * pltpu.roll(x, n - d, 1))
            pair_hi.append(h)
            pair_lo.append(l)
        table = jnp.concatenate(
            [jnp.concatenate(table_hi, axis=1), jnp.concatenate(table_lo, axis=1)], axis=0
        )
        acc[...] += lax.dot_general(
            jnp.concatenate(pair_hi, axis=1), table, ABT, preferred_element_type=F32
        ) + lax.dot_general(
            jnp.concatenate(pair_lo, axis=1), table, ABT, preferred_element_type=F32
        )
        return carry

    lax.fori_loop(0, -(-(half + 1) // GROUP), step, 0)
    out_ref[...] += acc[:, :n] + acc[:, n:]


def coagulate(dens, kernel, fragment_bins):
    cells, n = dens.shape
    return pl.pallas_call(
        coag_kernel,
        out_shape=jax.ShapeDtypeStruct((cells, n), F32),
        in_specs=[VMEM, VMEM, VMEM],
        out_specs=VMEM,
        scratch_shapes=[
            pltpu.VMEM((2, n, n), F32),
            pltpu.VMEM((2, n, n), F32),
            pltpu.VMEM((cells, 2 * n), F32),
        ],
        compiler_params=pltpu.CompilerParams(vmem_limit_bytes=48 * 2**20),
        cost_estimate=pl.CostEstimate(
            flops=4 * cells * n * n * n, bytes_accessed=8 * cells * n, transcendentals=0
        ),
        name="coagulate",
    )(dens, kernel, fragment_bins)


def turn_kernel(owned, per_cell, shifts_ref, x_ref, out_ref, twice):
    parts, _, rows, n = x_ref.shape
    whole = parts * rows
    first = lax.axis_index("az") * owned
    for c in range(owned):
        x = x_ref[:, c].reshape(whole, n)
        twice[c, :whole] = x
        twice[c, whole:] = x
        shift = shifts_ref[first + c] * per_cell
        out_ref[:, c] = twice[c, pl.ds(whole - shift, whole), :].reshape(parts, rows, n)


def turn(x, shifts, per_cell):
    parts, owned, rows, n = x.shape
    return pl.pallas_call(
        functools.partial(turn_kernel, owned, per_cell),
        out_shape=jax.ShapeDtypeStruct(x.shape, F32),
        in_specs=[SMEM, VMEM],
        out_specs=VMEM,
        scratch_shapes=[pltpu.VMEM((owned, 2 * parts * rows, n), F32)],
        compiler_params=pltpu.CompilerParams(vmem_limit_bytes=32 * 2**20),
        cost_estimate=pl.CostEstimate(flops=0, bytes_accessed=8 * x.size, transcendentals=0),
        name="turn",
    )(shifts, x)


def coarse_kernel(dens_ref, vel_ref, out_ref):
    fine = dens_ref.shape[1]
    cells = fine // 4
    q = lax.broadcasted_iota(jnp.int32, (fine, cells), 0)
    p = lax.broadcasted_iota(jnp.int32, (fine, cells), 1)
    pool = jnp.where(q // 4 == p, 0.25, 0.0)
    vel = vel_ref[...]
    parts = [dens_ref[...], vel[:, :fine], vel[:, fine:]]
    for i, x in enumerate(parts):
        out_ref[:, i * cells : (i + 1) * cells] = jnp.dot(
            x, pool, precision=lax.Precision.HIGHEST, preferred_element_type=F32
        )


def drag_kernel(
    map_ref, prev_ref, own_ref, grain_ref, coag_ref, vel_ref, vel_out_ref, back_ref, kick_ref
):
    cycles = map_ref.shape[1]
    gas_cycles = own_ref.shape[0]
    cells = own_ref.shape[1] // 3
    n = grain_ref.shape[1]
    first = (lax.axis_index("rad") - 1) * gas_cycles
    row = lax.broadcasted_iota(jnp.int32, (2 * gas_cycles, cycles), 0)
    select = jnp.where(map_ref[...] - first == row, 1.0, 0.0)
    near = jnp.concatenate([prev_ref[...], own_ref[...]], axis=0)
    gas = lax.dot_general(
        near.T, select, (((1,), (0,)), ((), ())),
        precision=lax.Precision.HIGHEST, preferred_element_type=F32,
    )
    grain = grain_ref[...]
    lane = lax.broadcasted_iota(jnp.int32, (cells, cycles), 1)
    moment = [jnp.zeros((cells, cycles), F32) for _ in range(2)]
    for r in range(cycles):
        rho = gas[:cells, r : r + 1]
        frac = 1.0 - jnp.exp(-rho / grain)
        dens = coag_ref[r * cells : (r + 1) * cells, :]
        for c in range(2):
            u = gas[(c + 1) * cells : (c + 2) * cells, r : r + 1]
            rows = pl.ds(r * 2 * cells + c, cells, 2)
            v = vel_ref[rows, :]
            new = v + (u - v) * frac
            vel_out_ref[rows, :] = new
            m = jnp.sum(dens * (new - v), axis=1, keepdims=True)
            moment[c] = jnp.where(lane == r, m, moment[c])
    both = jnp.concatenate(moment, axis=0) / n
    kick = lax.dot_general(
        both, select, ABT, precision=lax.Precision.HIGHEST, preferred_element_type=F32
    )
    back_ref[...] = kick[:, :gas_cycles]
    kick_ref[...] = kick[:, gas_cycles:]


def gas_kernel(kick_ref, from_next_ref, dens_ref, vel_ref, out_ref):
    fine = dens_ref.shape[1]
    cells = fine // 4
    kick = (kick_ref[...] + from_next_ref[...]).T
    p = lax.broadcasted_iota(jnp.int32, (cells, fine), 0)
    q = lax.broadcasted_iota(jnp.int32, (cells, fine), 1)
    spread = jnp.where(q // 4 == p, 1.0, 0.0)
    dens = dens_ref[...]
    for c in range(2):
        wide = jnp.dot(
            kick[:, c * cells : (c + 1) * cells], spread,
            precision=lax.Precision.HIGHEST, preferred_element_type=F32,
        )
        own = slice(c * fine, (c + 1) * fine)
        out_ref[:, own] = vel_ref[:, own] - wide / dens


def shifted(block, axis, distance):
    devices = range(lax.axis_size(axis))
    route = [(i - distance, i) for i in devices if i - distance in devices]
    return lax.ppermute(block, axis, route)


def exchange(x):
    return lax.all_to_all(x, "az", split_axis=0, concat_axis=0, tiled=True)


def body(
    dust_density,
    dust_velocity,
    gas_density,
    gas_velocity,
    kernel,
    grain_param,
    cycle_shifts,
    fragment_bins,
    gas_map,
):
    cycles, cells, bins = dust_density.shape
    gas_cycles, fine = gas_density.shape
    parts = lax.axis_size("az")
    owned = cycles // parts
    gas_flat = gas_velocity.reshape(gas_cycles, 2 * fine)

    vel = exchange(dust_velocity.reshape(parts, owned, 2 * cells, bins))
    coag = coagulate(dust_density.reshape(cycles * cells, bins), kernel, fragment_bins)
    coag = exchange(coag.reshape(parts, owned, cells, bins))
    vel = exchange(turn(vel, cycle_shifts, 2))
    coag = exchange(turn(coag, cycle_shifts, 1))

    coarse = pl.pallas_call(
        coarse_kernel,
        out_shape=jax.ShapeDtypeStruct((gas_cycles, 3 * cells), F32),
        name="coarse",
    )(gas_density, gas_flat)
    prev = shifted(coarse, "rad", 1)

    coag = coag.reshape(cycles * cells, bins)
    vel_out, back, kick = pl.pallas_call(
        drag_kernel,
        out_shape=(
            jax.ShapeDtypeStruct((2 * cycles * cells, bins), F32),
            jax.ShapeDtypeStruct((2 * cells, gas_cycles), F32),
            jax.ShapeDtypeStruct((2 * cells, gas_cycles), F32),
        ),
        compiler_params=pltpu.CompilerParams(vmem_limit_bytes=32 * 2**20),
        name="drag",
    )(
        gas_map.reshape(1, cycles),
        prev,
        coarse,
        grain_param.reshape(1, bins),
        coag,
        vel.reshape(2 * cycles * cells, bins),
    )
    from_next = shifted(back, "rad", -1)
    gas_out = pl.pallas_call(
        gas_kernel,
        out_shape=jax.ShapeDtypeStruct((gas_cycles, 2 * fine), F32),
        name="gas",
    )(kick, from_next, gas_density, gas_flat)
    return (
        coag.reshape(cycles, cells, bins),
        vel_out.reshape(cycles, cells, 2, bins),
        gas_out.reshape(gas_cycles, 2, fine),
    )


def solution(mesh):
    placed = (
        P("rad", "az", None),
        P("rad", "az", None, None),
        P("rad", "az"),
        P("rad", None, "az"),
        P(),
        P(),
        P("rad"),
        P(),
        P("rad"),
    )
    return jax.shard_map(
        body,
        mesh=mesh,
        in_specs=placed,
        out_specs=(P("rad", "az", None), P("rad", "az", None, None), P("rad", None, "az")),
        check_vma=False,
    )
```

time: 467 us -> 139 us (0.30)
  matrix products: 341 us -> 0 us
  Pallas kernels: 0 us -> 30.4 us
  other arithmetic: 24.5 us -> 0 us
  blocking collectives: 0 us -> 19.5 us
  waiting for transfers between devices: 69.4 us -> 57.2 us
    dot_general x35 -> x0, matrix products: 341 us -> none  [the longest x16 326 us: coag_block(): gain = jnp.dot(pairs, table, precision=lax.Precision.HIGHEST)]
    pallas_call x0 -> x6, Pallas kernels: none -> 30.4 us  [the longest x1 11.9 us: coagulate(): pl.pallas_call(coag_kernel, out_shape=jax.ShapeDtypeStruct((cells, n), F3...]
    all_to_all x0 -> x1, blocking collectives: none -> 19.5 us  [exchange(): return lax.all_to_all(x, 'az', split_axis=0, concat_axis=0, tiled=True)]
    mul x16 -> x0, other arithmetic: 18.3 us -> none  [coag_block(): pairs = (dens[:, :, None] * dens[:, None, :]).reshape(dens.shape[0], -1)]
    all_to_all x2 -> x3, waiting for transfers between devices: 65.2 us -> 50.6 us  [exchange(): return lax.all_to_all(x, 'az', split_axis=0, concat_axis=0, tiled=True)]
    gather x1 -> x0, local copies, waits for them, and re-layouts: 6.18 us -> none  [body(): turned = jnp.take_along_axis(whole, position[:, :, None, None], axis=1)]
    all_to_all x2 -> x3, starting transfers between devices: 11.6 us -> 15.5 us  [exchange(): return lax.all_to_all(x, 'az', split_axis=0, concat_axis=0, tiled=True)]
  transfers between devices with their start and end apart: 5 -> 5, of which waited for: 4 -> 5; matrix products, arithmetic and copies ran while one was open for 1% -> 1% of each run, Pallas kernels for 0% -> 4%
where the time goes in v1:
time: 139 us; the launch traced here: 137 us
  waiting for transfers between devices  57.2 us (41%)
  Pallas kernels  30.4 us (22%)
  starting transfers between devices  20.2 us (15%)
  blocking collectives  19.5 us (14%)
  local copies, waits for them, and re-layouts  9.35 us (7%)
    all_to_all x3, waiting for transfers between devices, exchange(): return lax.all_to_all(x, 'az', split_axis=0, concat_axis=0, tiled=True)  50.6 us
    all_to_all x1, blocking collectives, exchange(): return lax.all_to_all(x, 'az', split_axis=0, concat_axis=0, tiled=True)  19.5 us
    all_to_all x3, starting transfers between devices, exchange(): return lax.all_to_all(x, 'az', split_axis=0, concat_axis=0, tiled=True)  15.5 us
    pallas_call x1, Pallas kernels, coagulate(): pl.pallas_call(coag_kernel, out_shape=jax.ShapeDtypeStruct((cells, n), F3...  11.9 us
    pallas_call x1, Pallas kernels, body(): pl.pallas_call(drag_kernel, out_shape=(jax.ShapeDtypeStruct((2 * cycles *...  11.6 us
    unnamed x24, local copies, waits for them, and re-layouts  7.05 us
    ppermute x2, waiting for transfers between devices, shifted(): return lax.ppermute(block, axis, route)  6.53 us
    ppermute x2, starting transfers between devices, shifted(): return lax.ppermute(block, axis, route)  4.69 us
  transfers between devices with their start and end apart: 5, of which 5 were waited for; matrix products, arithmetic and copies ran while one was open for 1% of the time, Pallas kernels for 4%

profile of v1, /device:TPU:10, one launch (start us, length us, event | category | flops | bytes accessed | tf_op | source)
XLA Modules:
  0.0 137.3 jit_solution(3400099985609911211)
XLA Ops:
  0.6 0.0 copy-start.5
  0.6 1.0 copy-done.5
  1.7 0.8 copy-done.6
  2.5 0.8 copy-done.7
  3.4 11.9 %coagulate.1 = f32[1024,128]{1,0:T(8,128)S(1)} custom-call(f32[1024,128]{1,0:T(8,128)S(1)} %bitcast.17, f32[128,128]{1,0:T(8,128)S(1)} %copy-done.6, s32[128,128]{1,0:T(8,128)S(1)} %copy-done.7), custom_call_target="tpu_custom_call" | custom-call | flops 8589934592 | bytes 1048576 | tf_op jit(solution)/shard_map/coagulate/pallas_call | solution.py:89
  15.2 19.5 %all_to_all.20.x_ref = f32[16,4,16,128]{3,2,1,0:T(8,128)S(1)} all-to-all(f32[16,4,16,128]{3,2,1,0:T(8,128)S(1)} %bitcast.14), channel_id=1, replica_groups=mesh['rad'=2,'az'=16] {'az'}, dimensions={0} | all-to-all | bytes 1048576 | tf_op jit(solution)/shard_map/all_to_all | solution.py:209
  34.7 5.3 %all-to-all-start.2 = ((f32[16,4,32,128]{3,2,1,0:T(8,128)}), f32[16,4,32,128]{3,2,1,0:T(8,128)S(1)}, u32[]{:S(2)}, u32[]{:S(2)}) async-start(f32[16,4,32,128]{3,2,1,0:T(8,128)} %bitcast.7), calls=%async_computation.2 | async-start | bytes 2097152 | tf_op jit(solution)/shard_map/all_to_all | solution.py:209
  40.0 1.4 %turn.2 = f32[16,4,16,128]{3,2,1,0:T(8,128)} custom-call(s32[64]{0:T(128)S(1)} %copy-done.2, f32[16,4,16,128]{3,2,1,0:T(8,128)S(1)} %all_to_all.20.x_ref), custom_call_target="tpu_custom_call" | custom-call | bytes 1048576 | tf_op jit(solution)/shard_map/turn/pallas_call | solution.py:121
  41.4 23.3 %all-to-all-done.2.x_ref = f32[16,4,32,128]{3,2,1,0:T(8,128)S(1)} async-done(((f32[16,4,32,128]{3,2,1,0:T(8,128)}), f32[16,4,32,128]{3,2,1,0:T(8,128)S(1)}, u32[]{:S(2)}, u32[]{:S(2)}) %all-to-all-start.2) | async-done | bytes 1048608 | tf_op jit(solution)/shard_map/all_to_all | solution.py:209
  64.7 5.1 %all-to-all-start.1 = ((f32[16,4,16,128]{3,2,1,0:T(8,128)}), f32[16,4,16,128]{3,2,1,0:T(8,128)S(1)}, u32[]{:S(2)}, u32[]{:S(2)}) async-start(f32[16,4,16,128]{3,2,1,0:T(8,128)} %turn.2), calls=%async_computation.1 | async-start | bytes 1048576 | tf_op jit(solution)/shard_map/all_to_all | solution.py:209
  69.8 1.7 %turn.3 = f32[16,4,32,128]{3,2,1,0:T(8,128)} custom-call(s32[64]{0:T(128)S(1)} %copy-done.2, f32[16,4,32,128]{3,2,1,0:T(8,128)S(1)} %all-to-all-done.2.x_ref), custom_call_target="tpu_custom_call" | custom-call | bytes 2097152 | tf_op jit(solution)/shard_map/turn/pallas_call | solution.py:121
  71.5 11.7 %all-to-all-done.1 = f32[16,4,16,128]{3,2,1,0:T(8,128)S(1)} async-done(((f32[16,4,16,128]{3,2,1,0:T(8,128)}), f32[16,4,16,128]{3,2,1,0:T(8,128)S(1)}, u32[]{:S(2)}, u32[]{:S(2)}) %all-to-all-start.1) | async-done | bytes 524320 | tf_op jit(solution)/shard_map/all_to_all | solution.py:209
  83.2 5.1 %all-to-all-start.3 = ((f32[16,4,32,128]{3,2,1,0:T(8,128)}), f32[16,4,32,128]{3,2,1,0:T(8,128)S(1)}, u32[]{:S(2)}, u32[]{:S(2)}) async-start(f32[16,4,32,128]{3,2,1,0:T(8,128)} %turn.3), calls=%async_computation.3 | async-start | bytes 2097152 | tf_op jit(solution)/shard_map/all_to_all | solution.py:209
  88.4 0.0 copy-start.8
  88.4 0.7 copy.16.dens_ref
  89.1 0.1 copy-done.8
  89.2 0.7 copy.17.vel_ref
  89.9 1.9 %coarse.1.own_ref = f32[128,48]{1,0:T(8,128)} custom-call(f32[128,64]{1,0:T(8,128)} %copy.16.dens_ref, f32[128,128]{1,0:T(8,128)} %copy.17.vel_ref), custom_call_target="tpu_custom_call" | custom-call | tf_op jit(solution)/shard_map/coarse/pallas_call | solution.py:235
  91.8 3.4 %collective-permute-start = (f32[128,48]{1,0:T(8,128)}, f32[128,48]{1,0:T(8,128)S(1)}, u32[]{:S(2)}, u32[]{:S(2)}) collective-permute-start(f32[128,48]{1,0:T(8,128)} %coarse.1.own_ref), channel_id=1, source_target_pairs={{0,16},{1,17},{2,18},{3,19},{4,20},{5,21},{6,22},{7,23},{8,24},{9,... | collective-permute-start | bytes 73736 | tf_op jit(solution)/shard_map/ppermute | solution.py:205
  95.2 2.2 %collective-permute-done.prev_ref = f32[128,48]{1,0:T(8,128)S(1)} collective-permute-done((f32[128,48]{1,0:T(8,128)}, f32[128,48]{1,0:T(8,128)S(1)}, u32[]{:S(2)}, u32[]{:S(2)}) %collective-permute-start) | collective-permute-done | bytes 24608 | tf_op jit(solution)/shard_map/ppermute | solution.py:205
  97.4 15.6 %all-to-all-done.3 = f32[16,4,32,128]{3,2,1,0:T(8,128)S(1)} async-done(((f32[16,4,32,128]{3,2,1,0:T(8,128)}), f32[16,4,32,128]{3,2,1,0:T(8,128)S(1)}, u32[]{:S(2)}, u32[]{:S(2)}) %all-to-all-start.3) | async-done | bytes 1048608 | tf_op jit(solution)/shard_map/all_to_all | solution.py:209
  113.1 0.7 copy-done.3
  113.7 0.0 copy-done.4
  113.8 0.8 copy-done
  114.6 11.6 %drag.1 = (f32[2048,128]{1,0:T(8,128)}, f32[32,128]{1,0:T(8,128)S(1)}, f32[32,128]{1,0:T(8,128)S(1)}) custom-call(s32[1,64]{1,0:T(1,128)S(1)} %bitcast.15, f32[128,48]{1,0:T(8,128)S(1)} %collective-permute-done.prev_ref, f32[128,48]{1,0:T(8,128)S(1)} %copy-done, f32[1,128]{1,0:T(1,128)S(1)} %bitcast.16, f32[1024,128]{1,0:T(8,128)S(1)} %bitcast.11, ...), custom_call_target="tpu_custom_call" | custom-call | tf_op jit(solution)/shard_map/drag/pallas_call | solution.py:243
  126.1 0.6 copy-done.1
  126.7 1.3 collective-permute-start.1
  128.0 4.3 %collective-permute-done.1.from_next_ref = f32[32,128]{1,0:T(8,128)S(1)} collective-permute-done((f32[32,128]{1,0:T(8,128)S(1)}, f32[32,128]{1,0:T(8,128)S(1)}, u32[]{:S(2)}, u32[]{:S(2)}) %collective-permute-start.1) | collective-permute-done | bytes 16416 | tf_op jit(solution)/shard_map/ppermute | solution.py:205
  132.4 0.6 copy-done.10
  133.0 2.0 %gas.1 = f32[128,128]{1,0:T(8,128)} custom-call(f32[32,128]{1,0:T(8,128)} %copy-done.1, f32[32,128]{1,0:T(8,128)} %copy-done.10, f32[128,64]{1,0:T(8,128)} %copy.16.dens_ref, f32[128,128]{1,0:T(8,128)} %copy.17.vel_ref), custom_call_target="tpu_custom_call" | custom-call | tf_op jit(solution)/shard_map/gas/pallas_call | solution.py:261
  134.9 1.6 %copy.20 = f32[128,128]{0,1:T(8,128)} copy(f32[128,128]{1,0:T(8,128)} %gas.1) | data formatting | bytes 131072 | tf_op jit(solution)/shard_map/gas/pallas_call | solution.py:261
  136.5 0.8 copy.22
  (11 shorter events, 0.0 us)
Async XLA Ops:
  0.6 1.0 copy-start.5
  1.7 0.8 copy-start.6
  2.5 0.8 copy-start.7
  34.7 5.3 %copy-start.2 = (s32[64]{0:T(128)S(1)}, s32[64]{0:T(128)}, u32[]{:S(2)}) copy-start(s32[64]{0:T(128)} %shifts_ref.3) | copy-start | bytes 772
  34.7 30.0 %all-to-all-start.2 = ((f32[16,4,32,128]{3,2,1,0:T(8,128)}), f32[16,4,32,128]{3,2,1,0:T(8,128)S(1)}, u32[]{:S(2)}, u32[]{:S(2)}) async-start(f32[16,4,32,128]{3,2,1,0:T(8,128)} %bitcast.7), calls=%async_computation.2 | async-start | bytes 2097152 | tf_op jit(solution)/shard_map/all_to_all | solution.py:209
  64.7 18.5 %all-to-all-start.1 = ((f32[16,4,16,128]{3,2,1,0:T(8,128)}), f32[16,4,16,128]{3,2,1,0:T(8,128)S(1)}, u32[]{:S(2)}, u32[]{:S(2)}) async-start(f32[16,4,16,128]{3,2,1,0:T(8,128)} %turn.2), calls=%async_computation.1 | async-start | bytes 1048576 | tf_op jit(solution)/shard_map/all_to_all | solution.py:209
  71.5 16.9 %copy-start.9 = (f32[128,64]{0,1:T(8,128)S(1)}, f32[128,64]{0,1:T(8,128)}, u32[]{:S(2)}) copy-start(f32[128,64]{0,1:T(8,128)} %param.11) | copy-start | bytes 98308
  83.2 29.9 %all-to-all-start.3 = ((f32[16,4,32,128]{3,2,1,0:T(8,128)}), f32[16,4,32,128]{3,2,1,0:T(8,128)S(1)}, u32[]{:S(2)}, u32[]{:S(2)}) async-start(f32[16,4,32,128]{3,2,1,0:T(8,128)} %turn.3), calls=%async_computation.3 | async-start | bytes 2097152 | tf_op jit(solution)/shard_map/all_to_all | solution.py:209
  88.4 0.8 copy-start.8
  91.8 5.6 %collective-permute-start = (f32[128,48]{1,0:T(8,128)}, f32[128,48]{1,0:T(8,128)S(1)}, u32[]{:S(2)}, u32[]{:S(2)}) collective-permute-start(f32[128,48]{1,0:T(8,128)} %coarse.1.own_ref), channel_id=1, source_target_pairs={{0,16},{1,17},{2,18},{3,19},{4,20},{5,21},{6,22},{7,23},{8,24},{9,... | collective-permute-start | bytes 73736 | tf_op jit(solution)/shard_map/ppermute | solution.py:205
  113.1 0.7 copy-start.3
  113.1 0.7 copy-start.4
  113.8 0.8 copy-start
  126.1 0.6 copy-start.1
  126.7 5.6 %collective-permute-start.1 = (f32[32,128]{1,0:T(8,128)S(1)}, f32[32,128]{1,0:T(8,128)S(1)}, u32[]{:S(2)}, u32[]{:S(2)}) collective-permute-start(f32[32,128]{1,0:T(8,128)S(1)} %get-tuple-element.8), channel_id=1, source_target_pairs={{16,0},{17,1},{18,2},{19,3},{20,4},{21,5},{22,6},{23,7},{24,8},{25... | collective-permute-start | bytes 49160 | tf_op jit(solution)/shard_map/ppermute | solution.py:205
  132.4 0.6 copy-start.10

commit v2 on v1

--- a/solution.py
+++ b/solution.py
@@ -104,30 +104,103 @@
     )(dens, kernel, fragment_bins)
 
 
-def turn_kernel(owned, per_cell, shifts_ref, x_ref, out_ref, twice):
-    parts, _, rows, n = x_ref.shape
-    whole = parts * rows
-    first = lax.axis_index("az") * owned
-    for c in range(owned):
-        x = x_ref[:, c].reshape(whole, n)
-        twice[c, :whole] = x
-        twice[c, whole:] = x
-        shift = shifts_ref[first + c] * per_cell
-        out_ref[:, c] = twice[c, pl.ds(whole - shift, whole), :].reshape(parts, rows, n)
-
-
-def turn(x, shifts, per_cell):
-    parts, owned, rows, n = x.shape
+def move_kernel(
+    owned, shifts_ref, vel_ref, dens_ref, vel_out, dens_out,
+    vel_land, dens_land, vel_turned, dens_turned, vel_twice, dens_twice, send_sem, recv_sem,
+):
+    me = lax.axis_index("az")
+    parts = vel_ref.shape[0]
+    half = owned // 2
+    vel = (vel_ref, vel_land, vel_turned, vel_out, vel_twice, 2)
+    dens = (dens_ref, dens_land, dens_turned, dens_out, dens_twice, 1)
+    units = [vel + (0, half), vel + (half, owned - half), dens + (0, owned)]
+
+    barrier = pltpu.get_barrier_semaphore()
+
+    def greet(k, carry):
+        other = lax.rem(me + k, parts)
+        pl.semaphore_signal(
+            barrier, inc=1, device_id={"az": other}, device_id_type=pl.DeviceIdType.MESH
+        )
+        return carry
+
+    lax.fori_loop(1, parts, greet, 0)
+    pl.semaphore_wait(barrier, parts - 1)
+
+    def copy(phase, u, k):
+        source, land, turned, end, _, _, first, count = units[u]
+        src, dst = (source, land) if phase == 0 else (turned, end)
+        other = lax.rem(me + k, parts)
+        own = pl.ds(first, count)
+        return pltpu.make_async_remote_copy(
+            src_ref=src.at[other, own],
+            dst_ref=dst.at[me, own],
+            send_sem=send_sem.at[phase, u, k],
+            recv_sem=recv_sem.at[phase, u, k],
+            device_id={"az": other},
+            device_id_type=pl.DeviceIdType.MESH,
+        )
+
+    def each(act):
+        def step(k, carry):
+            act(k)
+            return carry
+
+        lax.fori_loop(1, parts, step, 0)
+
+    for u, (source, land, _, _, _, _, first, count) in enumerate(units):
+        each(lambda k: copy(0, u, k).start())
+        land[me, pl.ds(first, count)] = source[me, pl.ds(first, count)]
+
+    for u, (_, land, turned, end, twice, per_cell, first, count) in enumerate(units):
+        each(lambda k: copy(0, u, k).wait_recv())
+        rows, n = land.shape[2:]
+        whole = parts * rows
+        for c in range(first, first + count):
+            x = land[:, c].reshape(whole, n)
+            twice[c, :whole] = x
+            twice[c, whole:] = x
+            shift = shifts_ref[me * owned + c] * per_cell
+            turned[:, c] = twice[c, pl.ds(whole - shift, whole), :].reshape(parts, rows, n)
+        each(lambda k: copy(1, u, k).start())
+        end[me, pl.ds(first, count)] = turned[me, pl.ds(first, count)]
+
+    for u in range(len(units)):
+        each(lambda k: copy(1, u, k).wait_recv())
+    for phase in range(2):
+        for u in range(len(units)):
+            each(lambda k: copy(phase, u, k).wait_send())
+
+
+def move(vel, dens, shifts):
+    parts, owned, rows, n = vel.shape
+    cells = dens.shape[2]
     return pl.pallas_call(
-        functools.partial(turn_kernel, owned, per_cell),
-        out_shape=jax.ShapeDtypeStruct(x.shape, F32),
-        in_specs=[SMEM, VMEM],
-        out_specs=VMEM,
-        scratch_shapes=[pltpu.VMEM((owned, 2 * parts * rows, n), F32)],
-        compiler_params=pltpu.CompilerParams(vmem_limit_bytes=32 * 2**20),
-        cost_estimate=pl.CostEstimate(flops=0, bytes_accessed=8 * x.size, transcendentals=0),
-        name="turn",
-    )(shifts, x)
+        functools.partial(move_kernel, owned),
+        out_shape=(
+            jax.ShapeDtypeStruct(vel.shape, F32),
+            jax.ShapeDtypeStruct(dens.shape, F32),
+        ),
+        in_specs=[SMEM, VMEM, VMEM],
+        out_specs=(VMEM, VMEM),
+        scratch_shapes=[
+            pltpu.VMEM(vel.shape, F32),
+            pltpu.VMEM(dens.shape, F32),
+            pltpu.VMEM(vel.shape, F32),
+            pltpu.VMEM(dens.shape, F32),
+            pltpu.VMEM((owned, 2 * parts * rows, n), F32),
+            pltpu.VMEM((owned, 2 * parts * cells, n), F32),
+            pltpu.SemaphoreType.DMA((2, 3, parts)),
+            pltpu.SemaphoreType.DMA((2, 3, parts)),
+        ],
+        compiler_params=pltpu.CompilerParams(
+            collective_id=0, has_side_effects=True, vmem_limit_bytes=40 * 2**20
+        ),
+        cost_estimate=pl.CostEstimate(
+            flops=0, bytes_accessed=8 * (vel.size + dens.size), transcendentals=0
+        ),
+        name="move",
+    )(shifts, vel, dens)
 
 
 def coarse_kernel(dens_ref, vel_ref, out_ref):
@@ -205,10 +278,6 @@
     return lax.ppermute(block, axis, route)
 
 
-def exchange(x):
-    return lax.all_to_all(x, "az", split_axis=0, concat_axis=0, tiled=True)
-
-
 def body(
     dust_density,
     dust_velocity,
@@ -226,11 +295,12 @@
     owned = cycles // parts
     gas_flat = gas_velocity.reshape(gas_cycles, 2 * fine)
 
-    vel = exchange(dust_velocity.reshape(parts, owned, 2 * cells, bins))
     coag = coagulate(dust_density.reshape(cycles * cells, bins), kernel, fragment_bins)
-    coag = exchange(coag.reshape(parts, owned, cells, bins))
-    vel = exchange(turn(vel, cycle_shifts, 2))
-    coag = exchange(turn(coag, cycle_shifts, 1))
+    vel, coag = move(
+        dust_velocity.reshape(parts, owned, 2 * cells, bins),
+        coag.reshape(parts, owned, cells, bins),
+        cycle_shifts,
+    )
 
     coarse = pl.pallas_call(
         coarse_kernel,

time: 139 us -> 121 us (0.87)
  Pallas kernels: 30.4 us -> 102 us
  waiting for transfers between devices: 57.2 us -> 4.34 us
  blocking collectives: 19.5 us -> 0 us
  starting transfers between devices: 20.2 us -> 4.69 us
    pallas_call x2 -> x1, Pallas kernels: 3.17 us -> 75 us  [move(): pl.pallas_call(functools.partial(move_kernel, owned), out_shape=(jax.Shap...]
    all_to_all x3 -> x0, waiting for transfers between devices: 50.6 us -> none  [exchange(): return lax.all_to_all(x, 'az', split_axis=0, concat_axis=0, tiled=True)]
    all_to_all x1 -> x0, blocking collectives: 19.5 us -> none  [exchange(): return lax.all_to_all(x, 'az', split_axis=0, concat_axis=0, tiled=True)]
    all_to_all x3 -> x0, starting transfers between devices: 15.5 us -> none  [exchange(): return lax.all_to_all(x, 'az', split_axis=0, concat_axis=0, tiled=True)]
    ppermute x2, waiting for transfers between devices: 6.53 us -> 4.34 us  [shifted(): return lax.ppermute(block, axis, route)]
  transfers between devices with their start and end apart: 5 -> 2, of which waited for: 5 -> 1; matrix products, arithmetic and copies ran while one was open for 1% -> 0% of each run, Pallas kernels for 4% -> 72%
where the time goes in v2:
time: 121 us; the launch traced here: 120 us
  Pallas kernels  102 us (84%)
  local copies, waits for them, and re-layouts  8.15 us (7%)
  starting transfers between devices  4.69 us (4%)
  waiting for transfers between devices  4.34 us (4%)
    pallas_call x1, Pallas kernels, move(): pl.pallas_call(functools.partial(move_kernel, owned), out_shape=(jax.Shap...  75 us
    pallas_call x1, Pallas kernels, coagulate(): pl.pallas_call(coag_kernel, out_shape=jax.ShapeDtypeStruct((cells, n), F3...  11.9 us
    pallas_call x1, Pallas kernels, body(): pl.pallas_call(drag_kernel, out_shape=(jax.ShapeDtypeStruct((2 * cycles *...  11.5 us
    unnamed x24, local copies, waits for them, and re-layouts  5.85 us
    ppermute x2, starting transfers between devices, shifted(): return lax.ppermute(block, axis, route)  4.69 us
    ppermute x2, waiting for transfers between devices, shifted(): return lax.ppermute(block, axis, route)  4.34 us
  transfers between devices with their start and end apart: 2, of which 1 were waited for; matrix products, arithmetic and copies ran while one was open for 0% of the time, Pallas kernels for 72%

profile of v2, /device:TPU:10, one launch (start us, length us, event | category | flops | bytes accessed | tf_op | source)
XLA Modules:
  0.0 120.3 jit_solution(3363058421243322534)
XLA Ops:
  0.6 0.0 copy-start.9
  0.6 1.5 %copy.16.dens_ref = f32[128,64]{1,0:T(8,128)} copy(f32[128,64]{0,1:T(8,128)} %param.11) | data formatting | bytes 65536 | tf_op args[2]
  2.2 0.0 copy-done.9
  2.2 0.7 copy.17.vel_ref
  2.9 0.0 copy-start.7
  2.9 0.0 copy-start.8
  2.9 1.9 %coarse.1.own_ref = f32[128,48]{1,0:T(8,128)} custom-call(f32[128,64]{1,0:T(8,128)} %copy.16.dens_ref, f32[128,128]{1,0:T(8,128)} %copy.17.vel_ref), custom_call_target="tpu_custom_call" | custom-call | tf_op jit(solution)/shard_map/coarse/pallas_call | solution.py:305
  4.8 3.4 %collective-permute-start = (f32[128,48]{1,0:T(8,128)}, f32[128,48]{1,0:T(8,128)S(1)}, u32[]{:S(2)}, u32[]{:S(2)}) collective-permute-start(f32[128,48]{1,0:T(8,128)} %coarse.1.own_ref), channel_id=1, source_target_pairs={{0,16},{1,17},{2,18},{3,19},{4,20},{5,21},{6,22},{7,23},{8,24},{9,... | collective-permute-start | bytes 73736 | tf_op jit(solution)/shard_map/ppermute | solution.py:278
  8.2 0.0 copy-done.7
  8.2 0.0 copy-done.8
  8.3 0.0 copy-start.6
  8.3 1.0 copy-done.6
  9.3 0.0 copy-start
  9.3 11.9 %coagulate.1 = f32[1024,128]{1,0:T(8,128)S(1)} custom-call(f32[1024,128]{1,0:T(8,128)S(1)} %bitcast.18, f32[128,128]{1,0:T(8,128)S(1)} %copy-done.7, s32[128,128]{1,0:T(8,128)S(1)} %copy-done.8), custom_call_target="tpu_custom_call" | custom-call | flops 8589934592 | bytes 1048576 | tf_op jit(solution)/shard_map/coagulate/pallas_call | solution.py:89
  21.2 0.0 copy-start.3
  21.2 0.0 copy-done
  21.2 0.6 copy-done.3
  21.8 75.0 %move.1 = (f32[16,4,32,128]{3,2,1,0:T(8,128)S(1)}, f32[16,4,16,128]{3,2,1,0:T(8,128)S(1)}) custom-call(s32[64]{0:T(128)S(1)} %copy-done.3, f32[16,4,32,128]{3,2,1,0:T(8,128)S(1)} %bitcast.13, f32[16,4,16,128]{3,2,1,0:T(8,128)S(1)} %bitcast.15), custom_call_target="tpu_custom_call" | custom-call | bytes 3145728 | tf_op jit(solution)/shard_map/move/pallas_call | solution.py:178
  96.9 0.0 collective-permute-done.prev_ref
  96.9 0.0 copy-start.4
  96.9 0.0 copy-start.5
  96.9 0.0 copy-done.1
  96.9 0.6 copy-done.4
  97.6 0.0 copy-done.5
  97.6 11.5 %drag.1 = (f32[2048,128]{1,0:T(8,128)}, f32[32,128]{1,0:T(8,128)S(1)}, f32[32,128]{1,0:T(8,128)S(1)}) custom-call(s32[1,64]{1,0:T(1,128)S(1)} %bitcast.16, f32[128,48]{1,0:T(8,128)S(1)} %collective-permute-done.prev_ref, f32[128,48]{1,0:T(8,128)S(1)} %copy-done.1, f32[1,128]{1,0:T(1,128)S(1)} %bitcast.17, f32[1024,128]{1,0:T(8,128)S(1)} %bitcast.11, ...), custom_call_target="tpu_custom_call" | custom-call | tf_op jit(solution)/shard_map/drag/pallas_call | solution.py:313
  109.1 0.6 copy-done.2
  109.7 1.3 %collective-permute-start.1 = (f32[32,128]{1,0:T(8,128)S(1)}, f32[32,128]{1,0:T(8,128)S(1)}, u32[]{:S(2)}, u32[]{:S(2)}) collective-permute-start(f32[32,128]{1,0:T(8,128)S(1)} %get-tuple-element.12), channel_id=1, source_target_pairs={{16,0},{17,1},{18,2},{19,3},{20,4},{21,5},{22,6},{23,7},{24,8},{25... | collective-permute-start | bytes 49160 | tf_op jit(solution)/shard_map/ppermute | solution.py:278
  111.0 4.3 %collective-permute-done.1.from_next_ref = f32[32,128]{1,0:T(8,128)S(1)} collective-permute-done((f32[32,128]{1,0:T(8,128)S(1)}, f32[32,128]{1,0:T(8,128)S(1)}, u32[]{:S(2)}, u32[]{:S(2)}) %collective-permute-start.1) | collective-permute-done | bytes 16416 | tf_op jit(solution)/shard_map/ppermute | solution.py:278
  115.3 0.6 copy-done.10
  115.9 2.0 %gas.1 = f32[128,128]{1,0:T(8,128)} custom-call(f32[32,128]{1,0:T(8,128)} %copy-done.2, f32[32,128]{1,0:T(8,128)} %copy-done.10, f32[128,64]{1,0:T(8,128)} %copy.16.dens_ref, f32[128,128]{1,0:T(8,128)} %copy.17.vel_ref), custom_call_target="tpu_custom_call" | custom-call | tf_op jit(solution)/shard_map/gas/pallas_call | solution.py:331
  117.9 1.6 %copy.20 = f32[128,128]{0,1:T(8,128)} copy(f32[128,128]{1,0:T(8,128)} %gas.1) | data formatting | bytes 131072 | tf_op jit(solution)/shard_map/gas/pallas_call | solution.py:331
  119.5 0.8 copy.22
  (3 shorter events, 0.0 us)
Async XLA Ops:
  0.6 1.5 %copy-start.9 = (f32[128,2,64]{0,2,1:T(8,128)S(1)}, f32[128,2,64]{0,2,1:T(8,128)}, u32[]{:S(2)}) copy-start(f32[128,2,64]{0,2,1:T(8,128)} %param.12) | copy-start | bytes 196612
  2.9 5.3 %copy-start.7 = (f32[128,128]{1,0:T(8,128)S(1)}, f32[128,128]{1,0:T(8,128)}, u32[]{:S(2)}) copy-start(f32[128,128]{1,0:T(8,128)} %rate_ref.1) | copy-start | bytes 196612
  2.9 5.4 %copy-start.8 = (s32[128,128]{1,0:T(8,128)S(1)}, s32[128,128]{1,0:T(8,128)}, u32[]{:S(2)}) copy-start(s32[128,128]{1,0:T(8,128)} %bins_ref.1) | copy-start | bytes 196612
  4.8 92.1 %collective-permute-start = (f32[128,48]{1,0:T(8,128)}, f32[128,48]{1,0:T(8,128)S(1)}, u32[]{:S(2)}, u32[]{:S(2)}) collective-permute-start(f32[128,48]{1,0:T(8,128)} %coarse.1.own_ref), channel_id=1, source_target_pairs={{0,16},{1,17},{2,18},{3,19},{4,20},{5,21},{6,22},{7,23},{8,24},{9,... | collective-permute-start | bytes 73736 | tf_op jit(solution)/shard_map/ppermute | solution.py:278
  8.3 1.0 copy-start.6
  9.3 11.9 %copy-start = (f32[64,16,2,128]{3,2,1,0:T(2,128)S(1)}, f32[64,16,2,128]{3,2,1,0:T(2,128)}, u32[]{:S(2)}) copy-start(f32[64,16,2,128]{3,2,1,0:T(2,128)} %param.10) | copy-start | bytes 3145732
  21.2 0.7 copy-start.3
  21.8 75.1 %copy-start.1 = (f32[128,48]{1,0:T(8,128)S(1)}, f32[128,48]{1,0:T(8,128)}, u32[]{:S(2)}) copy-start(f32[128,48]{1,0:T(8,128)} %coarse.1.own_ref) | copy-start | bytes 73732
  96.9 0.7 copy-start.4
  96.9 0.7 copy-start.5
  109.1 0.6 copy-start.2
  109.7 5.6 %collective-permute-start.1 = (f32[32,128]{1,0:T(8,128)S(1)}, f32[32,128]{1,0:T(8,128)S(1)}, u32[]{:S(2)}, u32[]{:S(2)}) collective-permute-start(f32[32,128]{1,0:T(8,128)S(1)} %get-tuple-element.12), channel_id=1, source_target_pairs={{16,0},{17,1},{18,2},{19,3},{20,4},{21,5},{22,6},{23,7},{24,8},{25... | collective-permute-start | bytes 49160 | tf_op jit(solution)/shard_map/ppermute | solution.py:278
  115.3 0.6 copy-start.10

commit v3 on v2

--- a/solution.py
+++ b/solution.py
@@ -30,7 +30,7 @@
     return x
 
 
-def coag_kernel(dens_ref, rate_ref, bins_ref, out_ref, rates, places, acc):
+def coagulate(dens_ref, rate_ref, bins_ref, out_ref, rates, places, acc):
     n = rate_ref.shape[0]
     half = n // 2
     rate = rate_ref[...]
@@ -84,29 +84,9 @@
     out_ref[...] += acc[:, :n] + acc[:, n:]
 
 
-def coagulate(dens, kernel, fragment_bins):
-    cells, n = dens.shape
-    return pl.pallas_call(
-        coag_kernel,
-        out_shape=jax.ShapeDtypeStruct((cells, n), F32),
-        in_specs=[VMEM, VMEM, VMEM],
-        out_specs=VMEM,
-        scratch_shapes=[
-            pltpu.VMEM((2, n, n), F32),
-            pltpu.VMEM((2, n, n), F32),
-            pltpu.VMEM((cells, 2 * n), F32),
-        ],
-        compiler_params=pltpu.CompilerParams(vmem_limit_bytes=48 * 2**20),
-        cost_estimate=pl.CostEstimate(
-            flops=4 * cells * n * n * n, bytes_accessed=8 * cells * n, transcendentals=0
-        ),
-        name="coagulate",
-    )(dens, kernel, fragment_bins)
-
-
 def move_kernel(
-    owned, shifts_ref, vel_ref, dens_ref, vel_out, dens_out,
-    vel_land, dens_land, vel_turned, dens_turned, vel_twice, dens_twice, send_sem, recv_sem,
+    owned, shifts_ref, vel_ref, start_ref, rate_ref, bins_ref, vel_out, dens_out,
+    flat, dens_ref, rates, places, acc, vel_land, dens_land, vel_turned, dens_turned, vel_twice, dens_twice, send_sem, recv_sem,
 ):
     me = lax.axis_index("az")
     parts = vel_ref.shape[0]
@@ -149,6 +129,9 @@
         lax.fori_loop(1, parts, step, 0)
 
     for u, (source, land, _, _, _, _, first, count) in enumerate(units):
+        if source is dens_ref:
+            coagulate(start_ref, rate_ref, bins_ref, flat, rates, places, acc)
+            dens_ref[...] = flat[...].reshape(dens_ref.shape)
         each(lambda k: copy(0, u, k).start())
         land[me, pl.ds(first, count)] = source[me, pl.ds(first, count)]
 
@@ -172,35 +155,43 @@
             each(lambda k: copy(phase, u, k).wait_send())
 
 
-def move(vel, dens, shifts):
+def move(vel, dens, shifts, kernel, fragment_bins):
     parts, owned, rows, n = vel.shape
-    cells = dens.shape[2]
+    cells = rows // 2
+    moved = (parts, owned, cells, n)
     return pl.pallas_call(
         functools.partial(move_kernel, owned),
         out_shape=(
             jax.ShapeDtypeStruct(vel.shape, F32),
-            jax.ShapeDtypeStruct(dens.shape, F32),
+            jax.ShapeDtypeStruct(moved, F32),
         ),
-        in_specs=[SMEM, VMEM, VMEM],
+        in_specs=[SMEM, VMEM, VMEM, VMEM, VMEM],
         out_specs=(VMEM, VMEM),
         scratch_shapes=[
+            pltpu.VMEM(dens.shape, F32),
+            pltpu.VMEM(moved, F32),
+            pltpu.VMEM((2, n, n), F32),
+            pltpu.VMEM((2, n, n), F32),
+            pltpu.VMEM((dens.shape[0], 2 * n), F32),
             pltpu.VMEM(vel.shape, F32),
-            pltpu.VMEM(dens.shape, F32),
+            pltpu.VMEM(moved, F32),
             pltpu.VMEM(vel.shape, F32),
-            pltpu.VMEM(dens.shape, F32),
+            pltpu.VMEM(moved, F32),
             pltpu.VMEM((owned, 2 * parts * rows, n), F32),
             pltpu.VMEM((owned, 2 * parts * cells, n), F32),
             pltpu.SemaphoreType.DMA((2, 3, parts)),
             pltpu.SemaphoreType.DMA((2, 3, parts)),
         ],
         compiler_params=pltpu.CompilerParams(
-            collective_id=0, has_side_effects=True, vmem_limit_bytes=40 * 2**20
+            collective_id=0, has_side_effects=True, vmem_limit_bytes=48 * 2**20
         ),
         cost_estimate=pl.CostEstimate(
-            flops=0, bytes_accessed=8 * (vel.size + dens.size), transcendentals=0
+            flops=4 * dens.size * n * n,
+            bytes_accessed=8 * (vel.size + dens.size),
+            transcendentals=0,
         ),
         name="move",
-    )(shifts, vel, dens)
+    )(shifts, vel, dens, kernel, fragment_bins)
 
 
 def coarse_kernel(dens_ref, vel_ref, out_ref):
@@ -295,11 +286,12 @@
     owned = cycles // parts
     gas_flat = gas_velocity.reshape(gas_cycles, 2 * fine)
 
-    coag = coagulate(dust_density.reshape(cycles * cells, bins), kernel, fragment_bins)
     vel, coag = move(
         dust_velocity.reshape(parts, owned, 2 * cells, bins),
-        coag.reshape(parts, owned, cells, bins),
+        dust_density.reshape(cycles * cells, bins),
         cycle_shifts,
+        kernel,
+        fragment_bins,
     )
 
     coarse = pl.pallas_call(

time: 121 us -> 110 us (0.909)
  Pallas kernels: 102 us -> 90.5 us
    pallas_call x1 -> x0, Pallas kernels: 11.9 us -> none  [coagulate(): pl.pallas_call(coag_kernel, out_shape=jax.ShapeDtypeStruct((cells, n), F3...]
    unnamed x24, local copies, waits for them, and re-layouts: 5.85 us -> 7.07 us
  transfers between devices with their start and end apart: 2 -> 2, of which waited for: 1 -> 1; matrix products, arithmetic and copies ran while one was open for 0% -> 0% of each run, Pallas kernels for 72% -> 69%
where the time goes in v3:
time: 110 us
  Pallas kernels  90.5 us (82%)
  local copies, waits for them, and re-layouts  9.36 us (9%)
  starting transfers between devices  4.69 us (4%)
  waiting for transfers between devices  4.34 us (4%)
    pallas_call x1, Pallas kernels, move(): pl.pallas_call(functools.partial(move_kernel, owned), out_shape=(jax.Shap...  75.1 us
    pallas_call x1, Pallas kernels, body(): pl.pallas_call(drag_kernel, out_shape=(jax.ShapeDtypeStruct((2 * cycles *...  11.5 us
    unnamed x24, local copies, waits for them, and re-layouts  7.07 us
    ppermute x2, starting transfers between devices, shifted(): return lax.ppermute(block, axis, route)  4.69 us
    ppermute x2, waiting for transfers between devices, shifted(): return lax.ppermute(block, axis, route)  4.34 us
  transfers between devices with their start and end apart: 2, of which 1 were waited for; matrix products, arithmetic and copies ran while one was open for 0% of the time, Pallas kernels for 69%

profile of v3, /device:TPU:10, one launch (start us, length us, event | category | flops | bytes accessed | tf_op | source)
XLA Modules:
  0.0 109.7 jit_solution(10284397385360652818)
XLA Ops:
  0.6 0.0 copy-start.9
  0.6 1.5 %copy.16.dens_ref = f32[128,64]{1,0:T(8,128)} copy(f32[128,64]{0,1:T(8,128)} %param.11) | data formatting | bytes 65536 | tf_op args[2]
  2.2 0.0 copy-done.9
  2.2 0.7 copy.17.vel_ref
  2.9 0.0 copy-start.6
  2.9 0.0 copy-start.7
  2.9 1.9 %coarse.1.own_ref = f32[128,48]{1,0:T(8,128)} custom-call(f32[128,64]{1,0:T(8,128)} %copy.16.dens_ref, f32[128,128]{1,0:T(8,128)} %copy.17.vel_ref), custom_call_target="tpu_custom_call" | custom-call | tf_op jit(solution)/shard_map/coarse/pallas_call | solution.py:297
  4.8 3.4 %collective-permute-start = (f32[128,48]{1,0:T(8,128)}, f32[128,48]{1,0:T(8,128)S(1)}, u32[]{:S(2)}, u32[]{:S(2)}) collective-permute-start(f32[128,48]{1,0:T(8,128)} %coarse.1.own_ref), channel_id=1, source_target_pairs={{0,16},{1,17},{2,18},{3,19},{4,20},{5,21},{6,22},{7,23},{8,24},{9,... | collective-permute-start | bytes 73736 | tf_op jit(solution)/shard_map/ppermute | solution.py:269
  8.2 0.0 copy-start.8
  8.2 0.0 copy-done.6
  8.3 0.0 copy-done.7
  8.3 0.6 copy-done.8
  8.9 0.0 copy-start.4
  8.9 1.2 %copy-done.4 = f32[64,16,2,128]{3,2,1,0:T(2,128)S(1)} copy-done((f32[64,16,2,128]{3,2,1,0:T(2,128)S(1)}, f32[64,16,2,128]{3,2,1,0:T(2,128)}, u32[]{:S(2)}) %copy-start.4) | copy-done | bytes 1048600
  10.1 1.0 copy-done.5
  11.2 0.0 copy-start
  11.2 75.1 %move.1 = (f32[16,4,32,128]{3,2,1,0:T(8,128)S(1)}, f32[16,4,16,128]{3,2,1,0:T(8,128)S(1)}) custom-call(s32[64]{0:T(128)S(1)} %copy-done.8, f32[16,4,32,128]{3,2,1,0:T(8,128)S(1)} %bitcast.15, f32[1024,128]{1,0:T(8,128)S(1)} %bitcast.16, f32[128,128]{1,0:T(8,128)S(1)} %copy-done.6, s32[128,128]{1,0:T(8,128)S(1)} %copy-done.7), custom_call_target="tpu_custom_call" | custom-call | flops 8589934592 | bytes 3145728 | tf_op jit(solution)/shard_map/move/pallas_call | solution.py:162
  86.3 0.0 collective-permute-done.prev_ref
  86.3 0.0 copy-start.2
  86.3 0.0 copy-start.3
  86.3 0.0 copy-done
  86.3 0.6 copy-done.2
  86.9 0.0 copy-done.3
  86.9 11.5 %drag.1 = (f32[2048,128]{1,0:T(8,128)}, f32[32,128]{1,0:T(8,128)S(1)}, f32[32,128]{1,0:T(8,128)S(1)}) custom-call(s32[1,64]{1,0:T(1,128)S(1)} %bitcast.13, f32[128,48]{1,0:T(8,128)S(1)} %collective-permute-done.prev_ref, f32[128,48]{1,0:T(8,128)S(1)} %copy-done, f32[1,128]{1,0:T(1,128)S(1)} %bitcast.14, f32[1024,128]{1,0:T(8,128)S(1)} %bitcast.10, ...), custom_call_target="tpu_custom_call" | custom-call | tf_op jit(solution)/shard_map/drag/pallas_call | solution.py:305
  98.5 0.0 copy-start.1
  98.5 0.6 copy-done.1
  99.1 1.3 %collective-permute-start.1 = (f32[32,128]{1,0:T(8,128)S(1)}, f32[32,128]{1,0:T(8,128)S(1)}, u32[]{:S(2)}, u32[]{:S(2)}) collective-permute-start(f32[32,128]{1,0:T(8,128)S(1)} %get-tuple-element.12), channel_id=1, source_target_pairs={{16,0},{17,1},{18,2},{19,3},{20,4},{21,5},{22,6},{23,7},{24,8},{25... | collective-permute-start | bytes 49160 | tf_op jit(solution)/shard_map/ppermute | solution.py:269
  100.4 4.3 %collective-permute-done.1.from_next_ref = f32[32,128]{1,0:T(8,128)S(1)} collective-permute-done((f32[32,128]{1,0:T(8,128)S(1)}, f32[32,128]{1,0:T(8,128)S(1)}, u32[]{:S(2)}, u32[]{:S(2)}) %collective-permute-start.1) | collective-permute-done | bytes 16416 | tf_op jit(solution)/shard_map/ppermute | solution.py:269
  104.7 0.6 copy-done.10
  105.3 2.0 %gas.1 = f32[128,128]{1,0:T(8,128)} custom-call(f32[32,128]{1,0:T(8,128)} %copy-done.1, f32[32,128]{1,0:T(8,128)} %copy-done.10, f32[128,64]{1,0:T(8,128)} %copy.16.dens_ref, f32[128,128]{1,0:T(8,128)} %copy.17.vel_ref), custom_call_target="tpu_custom_call" | custom-call | tf_op jit(solution)/shard_map/gas/pallas_call | solution.py:323
  107.3 1.6 %copy.20 = f32[128,128]{0,1:T(8,128)} copy(f32[128,128]{1,0:T(8,128)} %gas.1) | data formatting | bytes 131072 | tf_op jit(solution)/shard_map/gas/pallas_call | solution.py:323
  108.9 0.8 copy.22
  (2 shorter events, 0.0 us)
Async XLA Ops:
  0.6 1.5 %copy-start.9 = (f32[128,2,64]{0,2,1:T(8,128)S(1)}, f32[128,2,64]{0,2,1:T(8,128)}, u32[]{:S(2)}) copy-start(f32[128,2,64]{0,2,1:T(8,128)} %param.12) | copy-start | bytes 196612
  2.9 5.4 %copy-start.6 = (f32[128,128]{1,0:T(8,128)S(1)}, f32[128,128]{1,0:T(8,128)}, u32[]{:S(2)}) copy-start(f32[128,128]{1,0:T(8,128)} %rate_ref.1) | copy-start | bytes 196612
  2.9 5.4 %copy-start.7 = (s32[128,128]{1,0:T(8,128)S(1)}, s32[128,128]{1,0:T(8,128)}, u32[]{:S(2)}) copy-start(s32[128,128]{1,0:T(8,128)} %bins_ref.1) | copy-start | bytes 196612
  4.8 81.4 %collective-permute-start = (f32[128,48]{1,0:T(8,128)}, f32[128,48]{1,0:T(8,128)S(1)}, u32[]{:S(2)}, u32[]{:S(2)}) collective-permute-start(f32[128,48]{1,0:T(8,128)} %coarse.1.own_ref), channel_id=1, source_target_pairs={{0,16},{1,17},{2,18},{3,19},{4,20},{5,21},{6,22},{7,23},{8,24},{9,... | collective-permute-start | bytes 73736 | tf_op jit(solution)/shard_map/ppermute | solution.py:269
  8.2 0.7 copy-start.8
  8.9 1.2 %copy-start.4 = (f32[64,16,2,128]{3,2,1,0:T(2,128)S(1)}, f32[64,16,2,128]{3,2,1,0:T(2,128)}, u32[]{:S(2)}) copy-start(f32[64,16,2,128]{3,2,1,0:T(2,128)} %param.10) | copy-start | bytes 3145732
  10.1 1.0 copy-start.5
  11.2 75.1 %copy-start = (f32[128,48]{1,0:T(8,128)S(1)}, f32[128,48]{1,0:T(8,128)}, u32[]{:S(2)}) copy-start(f32[128,48]{1,0:T(8,128)} %coarse.1.own_ref) | copy-start | bytes 73732
  86.3 0.7 copy-start.2
  86.3 0.7 copy-start.3
  98.5 0.6 copy-start.1
  99.1 5.6 %collective-permute-start.1 = (f32[32,128]{1,0:T(8,128)S(1)}, f32[32,128]{1,0:T(8,128)S(1)}, u32[]{:S(2)}, u32[]{:S(2)}) collective-permute-start(f32[32,128]{1,0:T(8,128)S(1)} %get-tuple-element.12), channel_id=1, source_target_pairs={{16,0},{17,1},{18,2},{19,3},{20,4},{21,5},{22,6},{23,7},{24,8},{25... | collective-permute-start | bytes 49160 | tf_op jit(solution)/shard_map/ppermute | solution.py:269
  104.7 0.6 copy-start.10

commit v4 on v3

--- a/solution.py
+++ b/solution.py
@@ -84,9 +84,30 @@
     out_ref[...] += acc[:, :n] + acc[:, n:]
 
 
+def beside(axis):
+    n = lax.axis_size(axis)
+    me = lax.axis_index(axis)
+    return lax.rem(me + n - 1, n), lax.rem(me + 1, n)
+
+
+def coarsen(dens_ref, vel_ref, out_ref):
+    fine = dens_ref.shape[1]
+    cells = fine // 4
+    q = lax.broadcasted_iota(jnp.int32, (fine, cells), 0)
+    p = lax.broadcasted_iota(jnp.int32, (fine, cells), 1)
+    pool = jnp.where((q >= 4 * p) & (q < 4 * p + 4), 0.25, 0.0)
+    vel = vel_ref[...]
+    parts = [dens_ref[...], vel[:, :fine], vel[:, fine:]]
+    for i, x in enumerate(parts):
+        out_ref[:, i * cells : (i + 1) * cells] = jnp.dot(
+            x, pool, precision=lax.Precision.HIGHEST, preferred_element_type=F32
+        )
+
+
 def move_kernel(
-    owned, shifts_ref, vel_ref, start_ref, rate_ref, bins_ref, vel_out, dens_out,
-    flat, dens_ref, rates, places, acc, vel_land, dens_land, vel_turned, dens_turned, vel_twice, dens_twice, send_sem, recv_sem,
+    owned, shifts_ref, vel_ref, start_ref, rate_ref, bins_ref, gas_dens_ref, gas_vel_ref,
+    vel_out, dens_out, coarse_ref, prev_ref,
+    flat, dens_ref, rates, places, acc, vel_land, dens_land, vel_turned, dens_turned, vel_twice, dens_twice, send_sem, recv_sem, gas_sem,
 ):
     me = lax.axis_index("az")
     parts = vel_ref.shape[0]
@@ -105,7 +126,19 @@
         return carry
 
     lax.fori_loop(1, parts, greet, 0)
-    pl.semaphore_wait(barrier, parts - 1)
+    before, after = beside("rad")
+    pl.semaphore_signal(
+        barrier, inc=1, device_id={"rad": before}, device_id_type=pl.DeviceIdType.MESH
+    )
+    pl.semaphore_wait(barrier, parts)
+    onward = pltpu.make_async_remote_copy(
+        src_ref=coarse_ref,
+        dst_ref=prev_ref,
+        send_sem=gas_sem.at[0],
+        recv_sem=gas_sem.at[1],
+        device_id={"rad": after},
+        device_id_type=pl.DeviceIdType.MESH,
+    )
 
     def copy(phase, u, k):
         source, land, turned, end, _, _, first, count = units[u]
@@ -130,6 +163,8 @@
 
     for u, (source, land, _, _, _, _, first, count) in enumerate(units):
         if source is dens_ref:
+            coarsen(gas_dens_ref, gas_vel_ref, coarse_ref)
+            onward.start()
             coagulate(start_ref, rate_ref, bins_ref, flat, rates, places, acc)
             dens_ref[...] = flat[...].reshape(dens_ref.shape)
         each(lambda k: copy(0, u, k).start())
@@ -153,20 +188,24 @@
     for phase in range(2):
         for u in range(len(units)):
             each(lambda k: copy(phase, u, k).wait_send())
-
-
-def move(vel, dens, shifts, kernel, fragment_bins):
+    onward.wait()
+
+
+def move(vel, dens, shifts, kernel, fragment_bins, gas_density, gas_flat):
     parts, owned, rows, n = vel.shape
     cells = rows // 2
     moved = (parts, owned, cells, n)
+    coarse = jax.ShapeDtypeStruct((gas_density.shape[0], 3 * cells), F32)
     return pl.pallas_call(
         functools.partial(move_kernel, owned),
         out_shape=(
             jax.ShapeDtypeStruct(vel.shape, F32),
             jax.ShapeDtypeStruct(moved, F32),
+            coarse,
+            coarse,
         ),
-        in_specs=[SMEM, VMEM, VMEM, VMEM, VMEM],
-        out_specs=(VMEM, VMEM),
+        in_specs=[SMEM] + [VMEM] * 6,
+        out_specs=(VMEM,) * 4,
         scratch_shapes=[
             pltpu.VMEM(dens.shape, F32),
             pltpu.VMEM(moved, F32),
@@ -181,6 +220,7 @@
             pltpu.VMEM((owned, 2 * parts * cells, n), F32),
             pltpu.SemaphoreType.DMA((2, 3, parts)),
             pltpu.SemaphoreType.DMA((2, 3, parts)),
+            pltpu.SemaphoreType.DMA((2,)),
         ],
         compiler_params=pltpu.CompilerParams(
             collective_id=0, has_side_effects=True, vmem_limit_bytes=48 * 2**20
@@ -191,21 +231,7 @@
             transcendentals=0,
         ),
         name="move",
-    )(shifts, vel, dens, kernel, fragment_bins)
-
-
-def coarse_kernel(dens_ref, vel_ref, out_ref):
-    fine = dens_ref.shape[1]
-    cells = fine // 4
-    q = lax.broadcasted_iota(jnp.int32, (fine, cells), 0)
-    p = lax.broadcasted_iota(jnp.int32, (fine, cells), 1)
-    pool = jnp.where(q // 4 == p, 0.25, 0.0)
-    vel = vel_ref[...]
-    parts = [dens_ref[...], vel[:, :fine], vel[:, fine:]]
-    for i, x in enumerate(parts):
-        out_ref[:, i * cells : (i + 1) * cells] = jnp.dot(
-            x, pool, precision=lax.Precision.HIGHEST, preferred_element_type=F32
-        )
+    )(shifts, vel, dens, kernel, fragment_bins, gas_density, gas_flat)
 
 
 def drag_kernel(
@@ -246,13 +272,29 @@
     kick_ref[...] = kick[:, gas_cycles:]
 
 
-def gas_kernel(kick_ref, from_next_ref, dens_ref, vel_ref, out_ref):
+def gas_kernel(kick_ref, back_ref, dens_ref, vel_ref, out_ref, from_next_ref, sems):
+    before, after = beside("rad")
+    barrier = pltpu.get_barrier_semaphore()
+    pl.semaphore_signal(
+        barrier, inc=1, device_id={"rad": after}, device_id_type=pl.DeviceIdType.MESH
+    )
+    pl.semaphore_wait(barrier, 1)
+    back = pltpu.make_async_remote_copy(
+        src_ref=back_ref,
+        dst_ref=from_next_ref,
+        send_sem=sems.at[0],
+        recv_sem=sems.at[1],
+        device_id={"rad": before},
+        device_id_type=pl.DeviceIdType.MESH,
+    )
+    back.start()
+    back.wait()
     fine = dens_ref.shape[1]
     cells = fine // 4
     kick = (kick_ref[...] + from_next_ref[...]).T
     p = lax.broadcasted_iota(jnp.int32, (cells, fine), 0)
     q = lax.broadcasted_iota(jnp.int32, (cells, fine), 1)
-    spread = jnp.where(q // 4 == p, 1.0, 0.0)
+    spread = jnp.where((q >= 4 * p) & (q < 4 * p + 4), 1.0, 0.0)
     dens = dens_ref[...]
     for c in range(2):
         wide = jnp.dot(
@@ -261,12 +303,6 @@
         )
         own = slice(c * fine, (c + 1) * fine)
         out_ref[:, own] = vel_ref[:, own] - wide / dens
-
-
-def shifted(block, axis, distance):
-    devices = range(lax.axis_size(axis))
-    route = [(i - distance, i) for i in devices if i - distance in devices]
-    return lax.ppermute(block, axis, route)
 
 
 def body(
@@ -286,20 +322,15 @@
     owned = cycles // parts
     gas_flat = gas_velocity.reshape(gas_cycles, 2 * fine)
 
-    vel, coag = move(
+    vel, coag, coarse, prev = move(
         dust_velocity.reshape(parts, owned, 2 * cells, bins),
         dust_density.reshape(cycles * cells, bins),
         cycle_shifts,
         kernel,
         fragment_bins,
-    )
-
-    coarse = pl.pallas_call(
-        coarse_kernel,
-        out_shape=jax.ShapeDtypeStruct((gas_cycles, 3 * cells), F32),
-        name="coarse",
-    )(gas_density, gas_flat)
-    prev = shifted(coarse, "rad", 1)
+        gas_density,
+        gas_flat,
+    )
 
     coag = coag.reshape(cycles * cells, bins)
     vel_out, back, kick = pl.pallas_call(
@@ -319,12 +350,18 @@
         coag,
         vel.reshape(2 * cycles * cells, bins),
     )
-    from_next = shifted(back, "rad", -1)
     gas_out = pl.pallas_call(
         gas_kernel,
         out_shape=jax.ShapeDtypeStruct((gas_cycles, 2 * fine), F32),
+        in_specs=[VMEM] * 4,
+        out_specs=VMEM,
+        scratch_shapes=[
+            pltpu.VMEM((2 * cells, gas_cycles), F32),
+            pltpu.SemaphoreType.DMA((2,)),
+        ],
+        compiler_params=pltpu.CompilerParams(collective_id=1, has_side_effects=True),
         name="gas",
-    )(kick, from_next, gas_density, gas_flat)
+    )(kick, back, gas_density, gas_flat)
     return (
         coag.reshape(cycles, cells, bins),
         vel_out.reshape(cycles, cells, 2, bins),

time: 110 us -> 102 us (0.927)
  starting transfers between devices: 4.69 us -> 0 us
  waiting for transfers between devices: 4.34 us -> 0 us
  Pallas kernels: 90.5 us -> 92.4 us
  local copies, waits for them, and re-layouts: 9.36 us -> 8.25 us
    ppermute x2 -> x0, starting transfers between devices: 4.69 us -> none  [shifted(): return lax.ppermute(block, axis, route)]
    ppermute x2 -> x0, waiting for transfers between devices: 4.34 us -> none  [shifted(): return lax.ppermute(block, axis, route)]
    pallas_call x1, Pallas kernels: 1.98 us -> 5.74 us  [body(): pl.pallas_call(gas_kernel, out_shape=jax.ShapeDtypeStruct((gas_cycles, 2...]
    pallas_call x1 -> x0, Pallas kernels: 1.92 us -> none  [body(): pl.pallas_call(coarse_kernel, out_shape=jax.ShapeDtypeStruct((gas_cycles,...]
    unnamed x24 -> x26, local copies, waits for them, and re-layouts: 7.07 us -> 6.59 us
  transfers between devices with their start and end apart: 2 -> 0, of which waited for: 1 -> 0; matrix products, arithmetic and copies ran while one was open for 0% -> 0% of each run, Pallas kernels for 69% -> 0%
where the time goes in v4:
time: 102 us; the launch traced here: 101 us
  Pallas kernels  92.4 us (91%)
  local copies, waits for them, and re-layouts  8.25 us (8%)
    pallas_call x1, Pallas kernels, move(): pl.pallas_call(functools.partial(move_kernel, owned), out_shape=(jax.Shap...  75.1 us
    pallas_call x1, Pallas kernels, body(): pl.pallas_call(drag_kernel, out_shape=(jax.ShapeDtypeStruct((2 * cycles *...  11.5 us
    unnamed x26, local copies, waits for them, and re-layouts  6.59 us
    pallas_call x1, Pallas kernels, body(): pl.pallas_call(gas_kernel, out_shape=jax.ShapeDtypeStruct((gas_cycles, 2...  5.74 us

profile of v4, /device:TPU:10, one launch (start us, length us, event | category | flops | bytes accessed | tf_op | source)
XLA Modules:
  0.0 101.4 jit_solution(7500617661186114509)
XLA Ops:
  0.6 0.0 copy-start.11
  0.6 0.0 copy-start.10
  0.7 0.9 copy.16.gas_dens_ref.dens_ref
  1.5 0.0 copy-done.11
  1.5 0.0 copy-start
  1.6 0.0 copy-start.8
  1.6 0.0 copy-start.9
  1.6 0.1 copy.17.gas_vel_ref.vel_ref
  1.7 0.0 copy-done.10
  1.7 0.7 copy-done.8
  2.4 0.0 copy-done.9
  2.5 0.0 copy-start.6
  2.5 1.2 %copy-done.6 = f32[64,16,2,128]{3,2,1,0:T(2,128)S(1)} copy-done((f32[64,16,2,128]{3,2,1,0:T(2,128)S(1)}, f32[64,16,2,128]{3,2,1,0:T(2,128)}, u32[]{:S(2)}) %copy-start.6) | copy-done | bytes 1048600
  3.7 0.0 copy-start.7
  3.7 1.0 %copy-done.7 = f32[64,16,128]{2,1,0:T(8,128)S(1)} copy-done((f32[64,16,128]{2,1,0:T(8,128)S(1)}, f32[64,16,128]{2,1,0:T(8,128)}, u32[]{:S(2)}) %copy-start.7) | copy-done | bytes 524312
  4.7 0.0 copy-start.1
  4.7 75.1 %move.1 = (f32[16,4,32,128]{3,2,1,0:T(8,128)S(1)}, f32[16,4,16,128]{3,2,1,0:T(8,128)S(1)}, f32[128,48]{1,0:T(8,128)S(1)}, f32[128,48]{1,0:T(8,128)S(1)}) custom-call(s32[64]{0:T(128)S(1)} %copy-done.10, f32[16,4,32,128]{3,2,1,0:T(8,128)S(1)} %bitcast.15, f32[1024,128]{1,0:T(8,128)S(1)} %bitcast.16, f32[128,128]{1,0:T(8,128)S(1)} %copy-done.8, ...), custom_call_target="tpu_custom_call" | custom-call | flops 8589934592 | bytes 3145728 | tf_op jit(solution)/shard_map/move/pallas_call | solution.py:199
  79.9 0.0 copy-done
  79.9 0.0 copy-done.1
  79.9 0.0 copy-start.4
  79.9 0.0 copy-start.5
  79.9 0.6 copy-done.4
  80.5 0.0 copy-done.5
  80.5 11.5 %drag.1 = (f32[2048,128]{1,0:T(8,128)}, f32[32,128]{1,0:T(8,128)S(1)}, f32[32,128]{1,0:T(8,128)S(1)}) custom-call(s32[1,64]{1,0:T(1,128)S(1)} %bitcast.13, f32[128,48]{1,0:T(8,128)S(1)} %get-tuple-element.11.prev_ref, f32[128,48]{1,0:T(8,128)S(1)} %get-tuple-element.12.own_ref, f32[1,128]{1,0:T(1,128)S(1)} %bitcast.14, f32[1024,128]{1,0:T(8,128)S(1)} %bitcast.10, ...), custom_call_target="tpu_custom_call" | custom-call | tf_op jit(solution)/shard_map/drag/pallas_call | solution.py:336
  92.1 0.0 copy-start.2
  92.1 0.6 copy-done.2
  92.7 0.0 copy-start.3
  92.7 0.6 copy-done.3
  93.3 5.7 %gas.1 = f32[128,128]{1,0:T(8,128)} custom-call(f32[32,128]{1,0:T(8,128)} %copy-done.3, f32[32,128]{1,0:T(8,128)} %copy-done.2, f32[128,64]{1,0:T(8,128)} %copy-done, f32[128,128]{1,0:T(8,128)} %copy-done.1), custom_call_target="tpu_custom_call" | custom-call | tf_op jit(solution)/shard_map/gas/pallas_call | solution.py:353
  99.0 1.6 %copy.20 = f32[128,128]{0,1:T(8,128)} copy(f32[128,128]{1,0:T(8,128)} %gas.1) | data formatting | bytes 131072 | tf_op jit(solution)/shard_map/gas/pallas_call | solution.py:353
  100.6 0.8 copy.22
Async XLA Ops:
  0.6 0.9 copy-start.11
  0.6 1.0 %copy-start.10 = (s32[64]{0:T(128)S(1)}, s32[64]{0:T(128)}, u32[]{:S(2)}) copy-start(s32[64]{0:T(128)} %shifts_ref.1) | copy-start | bytes 772
  1.5 78.3 %copy-start = (f32[128,64]{1,0:T(8,128)}, f32[128,64]{1,0:T(8,128)S(1)}, u32[]{:S(2)}) copy-start(f32[128,64]{1,0:T(8,128)S(1)} %copy.16.gas_dens_ref.dens_ref) | copy-start | bytes 98308
  1.6 0.9 copy-start.8
  1.6 0.9 copy-start.9
  2.5 1.2 %copy-start.6 = (f32[64,16,2,128]{3,2,1,0:T(2,128)S(1)}, f32[64,16,2,128]{3,2,1,0:T(2,128)}, u32[]{:S(2)}) copy-start(f32[64,16,2,128]{3,2,1,0:T(2,128)} %param.10) | copy-start | bytes 3145732
  3.7 1.0 %copy-start.7 = (f32[64,16,128]{2,1,0:T(8,128)S(1)}, f32[64,16,128]{2,1,0:T(8,128)}, u32[]{:S(2)}) copy-start(f32[64,16,128]{2,1,0:T(8,128)} %param.9) | copy-start | bytes 1572868
  4.7 75.1 %copy-start.1 = (f32[128,128]{1,0:T(8,128)}, f32[128,128]{1,0:T(8,128)S(1)}, u32[]{:S(2)}) copy-start(f32[128,128]{1,0:T(8,128)S(1)} %copy.17.gas_vel_ref.vel_ref) | copy-start | bytes 196612
  79.9 0.7 copy-start.4
  79.9 0.7 copy-start.5
  92.1 0.6 copy-start.2
  92.7 0.6 copy-start.3

commit v5 on v4

--- a/solution.py
+++ b/solution.py
@@ -1,4 +1,5 @@
 import functools
+import math
 
 import jax
 import jax.numpy as jnp
@@ -154,9 +155,11 @@
             device_id_type=pl.DeviceIdType.MESH,
         )
 
+    stride = next(m for m in range(max(parts // 2 - 1, 1), parts) if math.gcd(m, parts - 1) == 1)
+
     def each(act):
         def step(k, carry):
-            act(k)
+            act(1 + lax.rem((k - 1) * stride, parts - 1))
             return carry
 
         lax.fori_loop(1, parts, step, 0)

time: 102 us -> 104 us (1.020)
  the two profiles are of different devices: /device:TPU:10 before, /device:TPU:2 now
where the time goes in v5:
time: 104 us
  Pallas kernels  94.5 us (91%)
  local copies, waits for them, and re-layouts  8.25 us (8%)
    pallas_call x1, Pallas kernels, move(): pl.pallas_call(functools.partial(move_kernel, owned), out_shape=(jax.Shap...  77.2 us
    pallas_call x1, Pallas kernels, body(): pl.pallas_call(drag_kernel, out_shape=(jax.ShapeDtypeStruct((2 * cycles *...  11.5 us
    unnamed x26, local copies, waits for them, and re-layouts  6.59 us
    pallas_call x1, Pallas kernels, body(): pl.pallas_call(gas_kernel, out_shape=jax.ShapeDtypeStruct((gas_cycles, 2...  5.74 us

profile of v5, /device:TPU:2, one launch (start us, length us, event | category | flops | bytes accessed | tf_op | source)
XLA Modules:
  0.0 103.5 jit_solution(5152307608248953614)
XLA Ops:
  0.6 0.0 copy-start.11
  0.6 0.0 copy-start.10
  0.7 0.9 copy.16.gas_dens_ref.dens_ref
  1.5 0.0 copy-done.11
  1.5 0.0 copy-start
  1.6 0.0 copy-start.8
  1.6 0.0 copy-start.9
  1.6 0.1 copy.17.gas_vel_ref.vel_ref
  1.7 0.0 copy-done.10
  1.7 0.7 copy-done.8
  2.4 0.0 copy-done.9
  2.5 0.0 copy-start.6
  2.5 1.2 %copy-done.6 = f32[64,16,2,128]{3,2,1,0:T(2,128)S(1)} copy-done((f32[64,16,2,128]{3,2,1,0:T(2,128)S(1)}, f32[64,16,2,128]{3,2,1,0:T(2,128)}, u32[]{:S(2)}) %copy-start.6) | copy-done | bytes 1048600
  3.7 0.0 copy-start.7
  3.7 1.0 %copy-done.7 = f32[64,16,128]{2,1,0:T(8,128)S(1)} copy-done((f32[64,16,128]{2,1,0:T(8,128)S(1)}, f32[64,16,128]{2,1,0:T(8,128)}, u32[]{:S(2)}) %copy-start.7) | copy-done | bytes 524312
  4.7 0.0 copy-start.1
  4.7 77.2 %move.1 = (f32[16,4,32,128]{3,2,1,0:T(8,128)S(1)}, f32[16,4,16,128]{3,2,1,0:T(8,128)S(1)}, f32[128,48]{1,0:T(8,128)S(1)}, f32[128,48]{1,0:T(8,128)S(1)}) custom-call(s32[64]{0:T(128)S(1)} %copy-done.10, f32[16,4,32,128]{3,2,1,0:T(8,128)S(1)} %bitcast.15, f32[1024,128]{1,0:T(8,128)S(1)} %bitcast.16, f32[128,128]{1,0:T(8,128)S(1)} %copy-done.8, ...), custom_call_target="tpu_custom_call" | custom-call | flops 8589934592 | bytes 3145728 | tf_op jit(solution)/shard_map/move/pallas_call | solution.py:202
  82.0 0.0 copy-done
  82.0 0.0 copy-done.1
  82.0 0.0 copy-start.4
  82.0 0.0 copy-start.5
  82.0 0.6 copy-done.4
  82.7 0.0 copy-done.5
  82.7 11.5 %drag.1 = (f32[2048,128]{1,0:T(8,128)}, f32[32,128]{1,0:T(8,128)S(1)}, f32[32,128]{1,0:T(8,128)S(1)}) custom-call(s32[1,64]{1,0:T(1,128)S(1)} %bitcast.13, f32[128,48]{1,0:T(8,128)S(1)} %get-tuple-element.11.prev_ref, f32[128,48]{1,0:T(8,128)S(1)} %get-tuple-element.12.own_ref, f32[1,128]{1,0:T(1,128)S(1)} %bitcast.14, f32[1024,128]{1,0:T(8,128)S(1)} %bitcast.10, ...), custom_call_target="tpu_custom_call" | custom-call | tf_op jit(solution)/shard_map/drag/pallas_call | solution.py:339
  94.2 0.0 copy-start.2
  94.2 0.6 copy-done.2
  94.8 0.0 copy-start.3
  94.8 0.6 copy-done.3
  95.4 5.7 %gas.1 = f32[128,128]{1,0:T(8,128)} custom-call(f32[32,128]{1,0:T(8,128)} %copy-done.3, f32[32,128]{1,0:T(8,128)} %copy-done.2, f32[128,64]{1,0:T(8,128)} %copy-done, f32[128,128]{1,0:T(8,128)} %copy-done.1), custom_call_target="tpu_custom_call" | custom-call | tf_op jit(solution)/shard_map/gas/pallas_call | solution.py:356
  101.2 1.6 %copy.20 = f32[128,128]{0,1:T(8,128)} copy(f32[128,128]{1,0:T(8,128)} %gas.1) | data formatting | bytes 131072 | tf_op jit(solution)/shard_map/gas/pallas_call | solution.py:356
  102.7 0.8 copy.22
Async XLA Ops:
  0.6 0.9 copy-start.11
  0.6 1.0 %copy-start.10 = (s32[64]{0:T(128)S(1)}, s32[64]{0:T(128)}, u32[]{:S(2)}) copy-start(s32[64]{0:T(128)} %shifts_ref.1) | copy-start | bytes 772
  1.5 80.4 %copy-start = (f32[128,64]{1,0:T(8,128)}, f32[128,64]{1,0:T(8,128)S(1)}, u32[]{:S(2)}) copy-start(f32[128,64]{1,0:T(8,128)S(1)} %copy.16.gas_dens_ref.dens_ref) | copy-start | bytes 98308
  1.6 0.9 copy-start.8
  1.6 0.9 copy-start.9
  2.5 1.2 %copy-start.6 = (f32[64,16,2,128]{3,2,1,0:T(2,128)S(1)}, f32[64,16,2,128]{3,2,1,0:T(2,128)}, u32[]{:S(2)}) copy-start(f32[64,16,2,128]{3,2,1,0:T(2,128)} %param.10) | copy-start | bytes 3145732
  3.7 1.0 %copy-start.7 = (f32[64,16,128]{2,1,0:T(8,128)S(1)}, f32[64,16,128]{2,1,0:T(8,128)}, u32[]{:S(2)}) copy-start(f32[64,16,128]{2,1,0:T(8,128)} %param.9) | copy-start | bytes 1572868
  4.7 77.3 %copy-start.1 = (f32[128,128]{1,0:T(8,128)}, f32[128,128]{1,0:T(8,128)S(1)}, u32[]{:S(2)}) copy-start(f32[128,128]{1,0:T(8,128)S(1)} %copy.17.gas_vel_ref.vel_ref) | copy-start | bytes 196612
  82.0 0.7 copy-start.4
  82.0 0.7 copy-start.5
  94.2 0.6 copy-start.2
  94.8 0.6 copy-start.3
